TPU v7x, 256 devices: a whole 4x4x8 slice. The times are simulated.
256 devices in a mesh: rep: 32 (over x, z), fsdp: 8 (over y, core).
Axes of the slice: x: 4, y: 4, z: 8, core: 2. Of those that a mesh axis runs over, the one named last changes fastest.
Arguments:
- grad_parts: bfloat16 [32, 8, 2097152], P('rep', 'fsdp'), may hold values from -6 to 6
- momentum: float32 [32, 2097152], P('rep', 'fsdp'), may hold values from -6 to 6
- bands: int32 [32, 4096, 32], P('rep', 'fsdp'), may hold values from 0 to 63, as said below
- counts: int32 [32, 4096], P('rep', 'fsdp'), may hold values from 1 to 32
Outputs:
- new_momentum: float32 [32, 2097152], P('rep', 'fsdp')
- update: float32 [2097152], P('fsdp')
Inputs may be any that keep to these rules, and one draw needn't show every extreme that they name: `bands`: in each list the 32 entries are distinct frequencies; entries at positions counts and beyond are ignored.
All inputs are finite; a program needn't handle non-finite values.
Results may differ from a plain program's by a relative error of at most 0.013.
Values may be sent and summed in bfloat16 or wider, within the bound.
No kernel may reach another device: no remote copies, remote signals or barrier semaphores. Data moves between devices by JAX's collectives and lax.ppermute only.
A program may use at most 128 MiB of HBM per device.

v0:
```python
import math

import jax
import jax.numpy as jnp
from jax import lax
from jax.sharding import PartitionSpec as P

SEG = 64
GROUP = 8
KMAX = 32


HIGH = lax.Precision.HIGHEST


def cosine_table():
    freq = jnp.arange(SEG, dtype=jnp.int32)[:, None].astype(jnp.float32)
    point = jnp.arange(SEG, dtype=jnp.int32)[None, :].astype(jnp.float32)
    scale = jnp.where(
        freq == 0.0, jnp.float32(math.sqrt(1.0 / SEG)), jnp.float32(math.sqrt(2.0 / SEG))
    )
    return scale * jnp.cos(jnp.float32(math.pi) * (2.0 * point + 1.0) * freq / (2.0 * SEG))


def body(grad_parts, momentum, bands, counts):
    table = cosine_table()
    paired = jnp.kron(jnp.eye(2, dtype=jnp.float32), table)
    freqs = jnp.arange(SEG, dtype=jnp.int32)
    slots = jnp.arange(KMAX, dtype=jnp.int32)
    replicas = lax.axis_size("rep")
    holders = lax.axis_size("fsdp")
    factor = 1.0 / math.sqrt(replicas)
    pieces = grad_parts.reshape(holders, -1)
    received = lax.all_to_all(pieces, "fsdp", split_axis=0, concat_axis=0, tiled=True)
    grad = jnp.sum(received.astype(jnp.float32), axis=0)
    moment = 0.999 * momentum.reshape(-1) + grad
    blocks = moment.shape[0] // (GROUP * SEG)
    coeff = jnp.dot(moment.reshape(-1, 2 * SEG), paired.T, precision=HIGH).reshape(
        blocks, GROUP, SEG
    )
    lists = bands.reshape(blocks, KMAX)
    live = counts.reshape(blocks)
    onehot = (
        (lists[:, :, None] == freqs[None, None, :]) & (slots[None, :, None] < live[:, None, None])
    ).astype(jnp.float32)
    values = jnp.einsum("cgf,ckf->cgk", coeff, onehot, precision=HIGH).astype(jnp.bfloat16)
    sent = jnp.einsum("cgk,ckf->cgf", values.astype(jnp.float32), onehot, precision=HIGH)
    back = jnp.dot(sent.reshape(-1, 2 * SEG), paired, precision=HIGH).reshape(-1)
    new_momentum = (moment - back).reshape(momentum.shape)
    empty = jnp.zeros((blocks, GROUP, SEG), jnp.float32)
    piece_vals = lax.all_gather(values.reshape(blocks, GROUP * KMAX), "rep", axis=0, tiled=True)
    piece_lists = lax.all_gather(lists, "rep", axis=0, tiled=True)
    rows = piece_vals.shape[0]
    shards = rows // blocks
    batch = math.gcd(shards, 4)
    turns = shards // batch
    vals_all = piece_vals.reshape(turns, batch, blocks, GROUP, KMAX)
    lists_all = piece_lists.reshape(turns, batch, blocks, KMAX)

    def add_group(turn, acc):
        vals = lax.dynamic_index_in_dim(vals_all, turn, 0, keepdims=False)
        kept = lax.dynamic_index_in_dim(lists_all, turn, 0, keepdims=False)
        hot = (kept[:, :, :, None] == freqs[None, None, None, :]).astype(jnp.bfloat16)
        return acc + jnp.einsum("rcgk,rckf->cgf", vals, hot, preferred_element_type=jnp.float32)

    total = lax.fori_loop(0, turns, add_group, empty)
    update = jnp.dot(total.reshape(-1, 2 * SEG), paired, precision=HIGH).reshape(-1) * factor
    return (new_momentum, update)


def solution(mesh):
    placed = (P("rep", "fsdp", None), P("rep", "fsdp"), P("rep", "fsdp", None), P("rep", "fsdp"))
    return jax.shard_map(
        body, mesh=mesh, in_specs=placed, out_specs=(P("rep", "fsdp"), P("fsdp")), check_vma=False
    )
```

profile of v0, /device:TPU:24, one launch (start us, length us, event | category | flops | bytes accessed | tf_op | source)
XLA Modules:
  0.0 457.3 jit_solution(12709773233317980911)
XLA Ops:
  7.7 27.1 %reduce.1 = bf16[8,262144]{1,0:T(8,128)(2,1)} reduce(bf16[8,1,262144]{2,1,0:T(2,128)(2,1)} %bitcast.42, bf16[]{:T(256)} %broadcast.110), dimensions={1}, to_apply=%bitcast.reduce_sub_computation | reduce | bytes 8388610 | tf_op jit(solution)/shard_map/all_to_all | solution.py:34
  34.8 8.1 %reshape.190 = bf16[8,2,131072]{2,1,0:T(2,128)(2,1)} reshape(bf16[8,262144]{1,0:T(8,128)(2,1)} %reduce.1) | data formatting | bytes 8388608
  42.8 6.6 %all-to-all-start = ((bf16[8,2,131072]{2,1,0:T(2,128)(2,1)}), bf16[8,2,131072]{2,1,0:T(2,128)(2,1)}, u32[]{:S(2)}, u32[]{:S(2)}) async-start(bf16[8,2,131072]{2,1,0:T(2,128)(2,1)} %reshape.190), calls=%async_computation | async-start | bytes 8388608 | tf_op jit(solution)/shard_map/all_to_all | solution.py:34
  52.3 44.8 %all-to-all-done = bf16[8,2,131072]{2,1,0:T(2,128)(2,1)} async-done(((bf16[8,2,131072]{2,1,0:T(2,128)(2,1)}), bf16[8,2,131072]{2,1,0:T(2,128)(2,1)}, u32[]{:S(2)}, u32[]{:S(2)}) %all-to-all-start) | async-done | bytes 4194336 | tf_op jit(solution)/shard_map/all_to_all | solution.py:34
  97.1 8.8 %reshape.191 = bf16[8,1,262144]{2,1,0:T(2,128)(2,1)} reshape(bf16[8,2,131072]{2,1,0:T(2,128)(2,1)} %all-to-all-done) | data formatting | bytes 8388608
  105.9 12.1 %convert_reduce_fusion = f32[262144]{0:T(1024)S(1)} fusion(bf16[8,1,262144]{2,1,0:T(2,128)(2,1)} %reshape.191), kind=kLoop, calls=%fused_computation.9 | loop fusion | flops 3932160 | bytes 5242880 | tf_op jit(solution)/shard_map/reduce_sum | solution.py:35
  120.7 11.1 %fusion.17 = bf16[512,8,32]{2,1,0:T(8,128)(2,1)S(1)} fusion(f32[512,8,64]{2,1,0:T(8,128)} %reshape.180, s32[512,32]{1,0:T(8,128)S(1)} %copy.11, pred[512,32]{1,0:T(8,128)(4,1)S(1)} %iota_compare_fusion.5), kind=kOutput, calls=%fused_computation.19 | convolution fusion | flops 102891520 | bytes 1392640 | tf_op jit(solution)/shard_map/cgf,ckf->cgk/dot_general | solution.py:46
  133.2 8.0 %fusion.8 = f32[512,8,64]{2,1,0:T(8,128)} fusion(bf16[512,8,32]{2,1,0:T(8,128)(2,1)S(1)} %fusion.17, s32[512,32]{1,0:T(8,128)S(1)} %copy.11, pred[512,32]{1,0:T(8,128)(4,1)S(1)} %iota_compare_fusion.5), kind=kOutput, calls=%fused_computation.11 | convolution fusion | flops 18874368 | bytes 1392640 | tf_op jit(solution)/shard_map/cgk,ckf->cgf/dot_general | solution.py:47
  141.2 1.9 reshape.181
  143.1 1.9 fusion.23
  145.1 3.7 add_subtract_fusion
  148.7 2.7 reshape.185
  151.4 98.2 %all-gather.4.cloned.1.call-done = bf16[16384,256]{0,1:T(8,128)(2,1)} async-done(((bf16[512,256]{0,1:T(8,128)(2,1)}), bf16[16384,256]{0,1:T(8,128)(2,1)}) %all-gather.4.cloned.1.call-update) | async-done | bytes 8388624 | tf_op jit(solution)/shard_map/all_gather | solution.py:51
  249.7 14.5 %reshape.184 = bf16[8,4,512,8,32]{2,1,0,4,3:T(4,128)(2,1)} reshape(bf16[16384,256]{0,1:T(8,128)(2,1)} %all-gather.4.cloned.1.call-done) | data formatting | bytes 16777216 | tf_op jit(solution)/shard_map/reshape | solution.py:57
  264.1 182.5 %while.14 = (s32[]{:T(128)}, f32[512,8,64]{2,1,0:T(8,128)}, bf16[8,4,512,8,32]{2,1,0,4,3:T(4,128)(2,1)}, s32[8,4,512,32]{2,1,0,3:T(4,128)S(1)}, s32[]{:T(128)}, /*index=5*/s32[]{:T(128)}) while((s32[]{:T(128)}, f32[512,8,64]{2,1,0:T(8,128)}, bf16[8,4,512,8,32]{2,1,0,4,3:T(4,128)(2,1)}, s32[8,4,512,32]{2,1,0,3:T(4,128)S(1)}, ...), condition=%wide.region_2.3_spmd.clone, body=%wide.region_1.2_spmd.clone.sunk | while | flops 71827456 | bytes 8650839 | solution.py:66
  265.7 6.8 %copy.21 = bf16[1,4,512,8,32]{4,3,1,2,0:T(8,128)(2,1)} copy(bf16[1,4,512,8,32]{2,1,0,4,3:T(4,128)(2,1)S(1)} %constant_dynamic-slice_fusion.5) | data formatting | bytes 2097152 | tf_op jit(solution)/shard_map/while/body/eval_jaxpr/jit(dynamic_index_in_dim)/dynamic_slice | solution.py:61
  273.0 13.9 %bitcast_add_fusion.2 = f32[512,8,64]{2,1,0:T(8,128)} fusion(f32[512,8,64]{2,1,0:T(8,128)} %get-tuple-element.164, s32[4,512,32]{2,0,1:T(4,128)S(1)} %bitcast.40, bf16[1,4,512,8,32]{4,3,1,2,0:T(8,128)(2,1)} %copy.21, pred[]{:T(512)S(6)} %compare.3), kind=kOutput, calls=%fused_computation.5.clone.2 | convolution fusion | flops 71827456 | bytes 3407873 | tf_op jit(solution)/shard_map/while/body/eval_jaxpr/rcgk,rckf->cgf/dot_general | solution.py:64
  288.5 6.8 %copy.21 = bf16[1,4,512,8,32]{4,3,1,2,0:T(8,128)(2,1)} copy(bf16[1,4,512,8,32]{2,1,0,4,3:T(4,128)(2,1)S(1)} %constant_dynamic-slice_fusion.5) | data formatting | bytes 2097152 | tf_op jit(solution)/shard_map/while/body/eval_jaxpr/jit(dynamic_index_in_dim)/dynamic_slice | solution.py:61
  295.8 13.9 %bitcast_add_fusion.2 = f32[512,8,64]{2,1,0:T(8,128)} fusion(f32[512,8,64]{2,1,0:T(8,128)} %get-tuple-element.164, s32[4,512,32]{2,0,1:T(4,128)S(1)} %bitcast.40, bf16[1,4,512,8,32]{4,3,1,2,0:T(8,128)(2,1)} %copy.21, pred[]{:T(512)S(6)} %compare.3), kind=kOutput, calls=%fused_computation.5.clone.2 | convolution fusion | flops 71827456 | bytes 3407873 | tf_op jit(solution)/shard_map/while/body/eval_jaxpr/rcgk,rckf->cgf/dot_general | solution.py:64
  311.3 6.8 %copy.21 = bf16[1,4,512,8,32]{4,3,1,2,0:T(8,128)(2,1)} copy(bf16[1,4,512,8,32]{2,1,0,4,3:T(4,128)(2,1)S(1)} %constant_dynamic-slice_fusion.5) | data formatting | bytes 2097152 | tf_op jit(solution)/shard_map/while/body/eval_jaxpr/jit(dynamic_index_in_dim)/dynamic_slice | solution.py:61
  318.6 13.9 %bitcast_add_fusion.2 = f32[512,8,64]{2,1,0:T(8,128)} fusion(f32[512,8,64]{2,1,0:T(8,128)} %get-tuple-element.164, s32[4,512,32]{2,0,1:T(4,128)S(1)} %bitcast.40, bf16[1,4,512,8,32]{4,3,1,2,0:T(8,128)(2,1)} %copy.21, pred[]{:T(512)S(6)} %compare.3), kind=kOutput, calls=%fused_computation.5.clone.2 | convolution fusion | flops 71827456 | bytes 3407873 | tf_op jit(solution)/shard_map/while/body/eval_jaxpr/rcgk,rckf->cgf/dot_general | solution.py:64
  334.2 6.8 %copy.21 = bf16[1,4,512,8,32]{4,3,1,2,0:T(8,128)(2,1)} copy(bf16[1,4,512,8,32]{2,1,0,4,3:T(4,128)(2,1)S(1)} %constant_dynamic-slice_fusion.5) | data formatting | bytes 2097152 | tf_op jit(solution)/shard_map/while/body/eval_jaxpr/jit(dynamic_index_in_dim)/dynamic_slice | solution.py:61
  341.5 13.9 %bitcast_add_fusion.2 = f32[512,8,64]{2,1,0:T(8,128)} fusion(f32[512,8,64]{2,1,0:T(8,128)} %get-tuple-element.164, s32[4,512,32]{2,0,1:T(4,128)S(1)} %bitcast.40, bf16[1,4,512,8,32]{4,3,1,2,0:T(8,128)(2,1)} %copy.21, pred[]{:T(512)S(6)} %compare.3), kind=kOutput, calls=%fused_computation.5.clone.2 | convolution fusion | flops 71827456 | bytes 3407873 | tf_op jit(solution)/shard_map/while/body/eval_jaxpr/rcgk,rckf->cgf/dot_general | solution.py:64
  357.0 6.8 %copy.21 = bf16[1,4,512,8,32]{4,3,1,2,0:T(8,128)(2,1)} copy(bf16[1,4,512,8,32]{2,1,0,4,3:T(4,128)(2,1)S(1)} %constant_dynamic-slice_fusion.5) | data formatting | bytes 2097152 | tf_op jit(solution)/shard_map/while/body/eval_jaxpr/jit(dynamic_index_in_dim)/dynamic_slice | solution.py:61
  364.3 13.9 %bitcast_add_fusion.2 = f32[512,8,64]{2,1,0:T(8,128)} fusion(f32[512,8,64]{2,1,0:T(8,128)} %get-tuple-element.164, s32[4,512,32]{2,0,1:T(4,128)S(1)} %bitcast.40, bf16[1,4,512,8,32]{4,3,1,2,0:T(8,128)(2,1)} %copy.21, pred[]{:T(512)S(6)} %compare.3), kind=kOutput, calls=%fused_computation.5.clone.2 | convolution fusion | flops 71827456 | bytes 3407873 | tf_op jit(solution)/shard_map/while/body/eval_jaxpr/rcgk,rckf->cgf/dot_general | solution.py:64
  379.8 6.8 %copy.21 = bf16[1,4,512,8,32]{4,3,1,2,0:T(8,128)(2,1)} copy(bf16[1,4,512,8,32]{2,1,0,4,3:T(4,128)(2,1)S(1)} %constant_dynamic-slice_fusion.5) | data formatting | bytes 2097152 | tf_op jit(solution)/shard_map/while/body/eval_jaxpr/jit(dynamic_index_in_dim)/dynamic_slice | solution.py:61
  387.1 13.9 %bitcast_add_fusion.2 = f32[512,8,64]{2,1,0:T(8,128)} fusion(f32[512,8,64]{2,1,0:T(8,128)} %get-tuple-element.164, s32[4,512,32]{2,0,1:T(4,128)S(1)} %bitcast.40, bf16[1,4,512,8,32]{4,3,1,2,0:T(8,128)(2,1)} %copy.21, pred[]{:T(512)S(6)} %compare.3), kind=kOutput, calls=%fused_computation.5.clone.2 | convolution fusion | flops 71827456 | bytes 3407873 | tf_op jit(solution)/shard_map/while/body/eval_jaxpr/rcgk,rckf->cgf/dot_general | solution.py:64
  402.6 6.8 %copy.21 = bf16[1,4,512,8,32]{4,3,1,2,0:T(8,128)(2,1)} copy(bf16[1,4,512,8,32]{2,1,0,4,3:T(4,128)(2,1)S(1)} %constant_dynamic-slice_fusion.5) | data formatting | bytes 2097152 | tf_op jit(solution)/shard_map/while/body/eval_jaxpr/jit(dynamic_index_in_dim)/dynamic_slice | solution.py:61
  409.9 13.9 %bitcast_add_fusion.2 = f32[512,8,64]{2,1,0:T(8,128)} fusion(f32[512,8,64]{2,1,0:T(8,128)} %get-tuple-element.164, s32[4,512,32]{2,0,1:T(4,128)S(1)} %bitcast.40, bf16[1,4,512,8,32]{4,3,1,2,0:T(8,128)(2,1)} %copy.21, pred[]{:T(512)S(6)} %compare.3), kind=kOutput, calls=%fused_computation.5.clone.2 | convolution fusion | flops 71827456 | bytes 3407873 | tf_op jit(solution)/shard_map/while/body/eval_jaxpr/rcgk,rckf->cgf/dot_general | solution.py:64
  425.5 6.8 %copy.21 = bf16[1,4,512,8,32]{4,3,1,2,0:T(8,128)(2,1)} copy(bf16[1,4,512,8,32]{2,1,0,4,3:T(4,128)(2,1)S(1)} %constant_dynamic-slice_fusion.5) | data formatting | bytes 2097152 | tf_op jit(solution)/shard_map/while/body/eval_jaxpr/jit(dynamic_index_in_dim)/dynamic_slice | solution.py:61
  432.7 13.9 %bitcast_add_fusion.2 = f32[512,8,64]{2,1,0:T(8,128)} fusion(f32[512,8,64]{2,1,0:T(8,128)} %get-tuple-element.164, s32[4,512,32]{2,0,1:T(4,128)S(1)} %bitcast.40, bf16[1,4,512,8,32]{4,3,1,2,0:T(8,128)(2,1)} %copy.21, pred[]{:T(512)S(6)} %compare.3), kind=kOutput, calls=%fused_computation.5.clone.2 | convolution fusion | flops 71827456 | bytes 3407873 | tf_op jit(solution)/shard_map/while/body/eval_jaxpr/rcgk,rckf->cgf/dot_general | solution.py:64
  448.5 1.9 fusion.16
  (52 shorter events, 25.4 us)
Async XLA Ops:
  42.8 7.5 %copy-start = (f32[1,262144]{1,0:T(1,128)S(1)}, f32[1,262144]{1,0:T(1,128)}, u32[]{:S(2)}) copy-start(f32[1,262144]{1,0:T(1,128)} %param.7) | copy-start | bytes 3145732
  42.8 54.2 %all-to-all-start = ((bf16[8,2,131072]{2,1,0:T(2,128)(2,1)}), bf16[8,2,131072]{2,1,0:T(2,128)(2,1)}, u32[]{:S(2)}, u32[]{:S(2)}) async-start(bf16[8,2,131072]{2,1,0:T(2,128)(2,1)} %reshape.190), calls=%async_computation | async-start | bytes 8388608 | tf_op jit(solution)/shard_map/all_to_all | solution.py:34
  49.4 2.6 copy-start.2
  49.4 2.7 copy-start.3
  49.4 99.3 %all-gather.6.cloned.1.call-start = ((), (), s32[]{:S(2)}) async-start(), calls=%async_computation.2 | async-start | bytes 2162688 | tf_op jit(solution)/shard_map/all_gather | solution.py:52
  50.1 199.5 %all-gather.4.cloned.1.call-start = ((), (), s32[]{:S(2)}) async-start(), calls=%async_computation.1 | async-start | bytes 8650752 | tf_op jit(solution)/shard_map/all_gather | solution.py:51
  141.2 3.9 copy-start.1
Sparse Core Ops, SparseCore 0:
  52.8 79.0 all-gather.5
  145.2 104.4 all-gather.3
where the time goes:
time: 459 us; the launch traced here: 457 us
  waiting for transfers between devices  144 us (31%)
  matrix products  135 us (29%)
  local copies, waits for them, and re-layouts  113 us (25%)
  other arithmetic  44.4 us (10%)
  between operations  14.2 us (3%)
  starting transfers between devices  6.82 us (1%)
    dot_general x8, matrix products, add_group(): jnp.einsum('rcgk,rckf->cgf', vals, hot, preferred_element_type=jnp.float32)  111 us
    all_gather x1, waiting for transfers between devices, body(): lax.all_gather(values.reshape(blocks, GROUP * KMAX), 'rep', axis=0, tiled...  98.2 us
    dynamic_slice x16, local copies, waits for them, and re-layouts, add_group(): vals = lax.dynamic_index_in_dim(vals_all, turn, 0, keepdims=False)  67.5 us
    all_to_all x1, waiting for transfers between devices, body(): lax.all_to_all(pieces, 'fsdp', split_axis=0, concat_axis=0, tiled=True)  44.8 us
    all_to_all x1, other arithmetic, body(): lax.all_to_all(pieces, 'fsdp', split_axis=0, concat_axis=0, tiled=True)  27.1 us
    unnamed x10, local copies, waits for them, and re-layouts  16.9 us
    reshape x1, local copies, waits for them, and re-layouts, body(): vals_all = piece_vals.reshape(turns, batch, blocks, GROUP, KMAX)  14.5 us
    reduce_sum x1, other arithmetic, body(): grad = jnp.sum(received.astype(jnp.float32), axis=0)  12.1 us
  transfers between devices with their start and end apart: 3, of which 2 were waited for; matrix products, arithmetic and copies ran while one was open for 12% of the time, Pallas kernels for 0%

commit v1 on v0

v1 whole, which is shorter than its diff:
```python
import math

import jax
import jax.numpy as jnp
import numpy as np
from jax import lax
from jax.experimental import pallas as pl
from jax.experimental.pallas import tpu as pltpu
from jax.sharding import PartitionSpec as P

SEG = 64
GROUP = 8
KMAX = 32
LANES = 128

HIGH = lax.Precision.HIGHEST
BF16 = jnp.bfloat16
F32 = jnp.float32


def paired_table():
    freq = np.arange(SEG, dtype=np.float64)[:, None]
    point = np.arange(SEG, dtype=np.float64)[None, :]
    scale = np.where(freq == 0.0, math.sqrt(1.0 / SEG), math.sqrt(2.0 / SEG))
    table = scale * np.cos(math.pi * (2.0 * point + 1.0) * freq / (2.0 * SEG))
    return np.kron(np.eye(2), table).astype(np.float32)


def unpack_pieces(raw, order):
    count = order.shape[0]
    size = raw.shape[-1] // 8
    rows = size // LANES
    step = min(rows, 128)

    def kernel(order_ref, raw_ref, *refs):
        outs, (held, dense, sem_in, sem_out) = refs[:count], refs[count:]

        def fetch(i):
            at = pl.multiple_of(order_ref[i] * size, size)
            return pltpu.make_async_copy(
                raw_ref.at[:, :, pl.ds(at, size)], held.at[i], sem_in.at[i]
            )

        def store(i):
            return pltpu.make_async_copy(dense.at[i], outs[i], sem_out.at[i])

        for i in range(count):
            fetch(i).start()
        for i in range(count):
            fetch(i).wait()

            @pl.loop(0, rows // step)
            def _(j):
                some = held[i, 0, :, pl.ds(pl.multiple_of(j * step * LANES, step * LANES), step * LANES)]
                dense[i, pl.ds(pl.multiple_of(j * step, step), step), :] = some.reshape(step, LANES)

            store(i).start()
        for i in range(count):
            store(i).wait()

    return pl.pallas_call(
        kernel,
        in_specs=[pl.BlockSpec(memory_space=pltpu.SMEM), pl.BlockSpec(memory_space=pl.ANY)],
        out_specs=[pl.BlockSpec(memory_space=pl.ANY)] * count,
        out_shape=[jax.ShapeDtypeStruct((rows, LANES), BF16)] * count,
        scratch_shapes=[
            pltpu.VMEM((count, 1, 1, size), BF16),
            pltpu.VMEM((count, rows, LANES), BF16),
            pltpu.SemaphoreType.DMA((count,)),
            pltpu.SemaphoreType.DMA((count,)),
        ],
        compiler_params=pltpu.CompilerParams(vmem_limit_bytes=24 << 20),
        cost_estimate=pl.CostEstimate(flops=0, bytes_accessed=count * size * 6, transcendentals=0),
    )(order, raw)


def transform_step(terms, momentum, mask, paired):
    rows = momentum.shape[0]
    step = min(rows, 512)

    def kernel(*refs):
        parts, (mom_ref, mask_ref, fwd_ref, inv_ref, sent_ref, new_ref) = refs[:-6], refs[-6:]
        grad = parts[0][...].astype(F32)
        for part in parts[1:]:
            grad = grad + part[...].astype(F32)
        moment = 0.999 * mom_ref[...] + grad
        coeff = jnp.dot(moment, fwd_ref[...], precision=HIGH, preferred_element_type=F32)
        sent = jnp.where(mask_ref[...].astype(F32) > 0.5, coeff, 0.0).astype(BF16)
        sent_ref[...] = sent
        back = jnp.dot(sent.astype(F32), inv_ref[...], precision=HIGH, preferred_element_type=F32)
        new_ref[...] = moment - back

    block = pl.BlockSpec((step, LANES), lambda i: (i, 0))
    whole = pl.BlockSpec((LANES, LANES), lambda i: (0, 0))
    return pl.pallas_call(
        kernel,
        grid=(rows // step,),
        in_specs=[block] * (len(terms) + 2) + [whole] * 2,
        out_specs=[block] * 2,
        out_shape=[
            jax.ShapeDtypeStruct((rows, LANES), BF16),
            jax.ShapeDtypeStruct((rows, LANES), F32),
        ],
        compiler_params=pltpu.CompilerParams(vmem_limit_bytes=24 << 20),
        cost_estimate=pl.CostEstimate(
            flops=rows * LANES * LANES * 24, bytes_accessed=rows * LANES * 24, transcendentals=0
        ),
    )(*terms, momentum, mask, jnp.asarray(paired.T), jnp.asarray(paired))


def combine_step(pieces, paired, factor):
    count, rows, _ = pieces.shape

    def kernel(pieces_ref, inv_ref, out_ref):
        total = jnp.sum(pieces_ref[...].astype(F32), axis=0)
        back = jnp.dot(total, inv_ref[...], precision=HIGH, preferred_element_type=F32)
        out_ref[...] = jnp.broadcast_to((back * factor).astype(BF16)[None], out_ref.shape)

    return pl.pallas_call(
        kernel,
        out_shape=jax.ShapeDtypeStruct(pieces.shape, BF16),
        compiler_params=pltpu.CompilerParams(vmem_limit_bytes=24 << 20),
        cost_estimate=pl.CostEstimate(
            flops=pieces.size, bytes_accessed=pieces.size * 4, transcendentals=0
        ),
    )(pieces, jnp.asarray(paired))


def body(grad_parts, momentum, bands, counts):
    replicas = lax.axis_size("rep")
    holders = lax.axis_size("fsdp")
    chips = holders // 2
    me = lax.axis_index("fsdp")
    core = me % 2
    chip = me // 2
    paired = paired_table()

    blocks = momentum.size // (GROUP * SEG)
    rows = momentum.size // LANES

    ahead = (chip + jnp.array([1, 2, 3, 0], jnp.int32)) % chips
    theirs = unpack_pieces(grad_parts, 2 * ahead + (1 - core))
    mine = unpack_pieces(grad_parts, 2 * ahead + core)
    swap = [(f, f ^ 1) for f in range(holders)]
    given = [lax.ppermute(t, "fsdp", swap) for t in theirs]

    def hop(n):
        return [(2 * c + k, 2 * ((c + n) % chips) + k) for c in range(chips) for k in range(2)]

    terms = [mine[3], given[3]]
    for i, n in enumerate((1, 2, 3)):
        both = (mine[i].astype(F32) + given[i].astype(F32)).astype(BF16)
        terms.append(lax.ppermute(both, "fsdp", hop(n)))

    freqs = jnp.arange(SEG, dtype=jnp.int32)
    slots = jnp.arange(KMAX, dtype=jnp.int32)
    lists = bands.reshape(blocks, KMAX)
    live = counts.reshape(blocks)
    hot = jnp.any(
        (lists[:, :, None] == freqs[None, None, :]) & (slots[None, :, None] < live[:, None, None]),
        axis=1,
    ).astype(BF16)
    mask = jnp.broadcast_to(
        jnp.concatenate([hot, hot], axis=1)[:, None, :], (blocks, GROUP // 2, LANES)
    ).reshape(rows, LANES)

    sent, new = transform_step(terms, momentum.reshape(rows, LANES), mask, paired)
    each = lax.all_to_all(
        sent.reshape(replicas, rows // replicas, LANES), "rep", split_axis=0, concat_axis=0, tiled=True
    )
    mixed = combine_step(each, paired, 1.0 / math.sqrt(replicas))
    update = lax.all_to_all(mixed, "rep", split_axis=0, concat_axis=0, tiled=True)
    return (new.reshape(momentum.shape), update.astype(F32).reshape(-1))


def solution(mesh):
    placed = (P("rep", "fsdp", None), P("rep", "fsdp"), P("rep", "fsdp", None), P("rep", "fsdp"))
    return jax.shard_map(
        body, mesh=mesh, in_specs=placed, out_specs=(P("rep", "fsdp"), P("fsdp")), check_vma=False
    )
```

time: 459 us -> 102 us (0.22)
  matrix products: 135 us -> 0 us
  waiting for transfers between devices: 144 us -> 23.9 us
  local copies, waits for them, and re-layouts: 113 us -> 3.67 us
  blocking collectives: 0 us -> 48.4 us
  other arithmetic: 44.4 us -> 5.38 us
  Pallas kernels: 0 us -> 14.4 us
  between operations: 14.2 us -> 0.8 us
    dot_general x13 -> x0, matrix products: 135 us -> none  [the longest x8 111 us: add_group(): jnp.einsum('rcgk,rckf->cgf', vals, hot, preferred_element_type=jnp.float32)]
    all_gather x2 -> x0, waiting for transfers between devices: 98.2 us -> none  [the longest x1 98.2 us: body(): lax.all_gather(values.reshape(blocks, GROUP * KMAX), 'rep', axis=0, tiled...]
    dynamic_slice x32 -> x0, local copies, waits for them, and re-layouts: 70.9 us -> none  [the longest x16 67.5 us: add_group(): vals = lax.dynamic_index_in_dim(vals_all, turn, 0, keepdims=False)]
    all_to_all x0 -> x2, blocking collectives: none -> 48.4 us  [the longest x1 26.3 us: body(): lax.all_to_all(sent.reshape(replicas, rows // replicas, LANES), 'rep', sp...]
    all_to_all x1 -> x0, waiting for transfers between devices: 44.8 us -> none  [body(): lax.all_to_all(pieces, 'fsdp', split_axis=0, concat_axis=0, tiled=True)]
    all_to_all x1 -> x0, other arithmetic: 27.1 us -> none  [body(): lax.all_to_all(pieces, 'fsdp', split_axis=0, concat_axis=0, tiled=True)]
    ppermute x0 -> x7, waiting for transfers between devices: none -> 23.9 us  [the longest x3 23.9 us: body(): terms.append(lax.ppermute(both, 'fsdp', hop(n)))]
    reshape x5 -> x0, local copies, waits for them, and re-layouts: 22.5 us -> none  [the longest x1 14.5 us: body(): vals_all = piece_vals.reshape(turns, batch, blocks, GROUP, KMAX)]
  transfers between devices with their start and end apart: 3 -> 7, of which waited for: 2 -> 2; matrix products, arithmetic and copies ran while one was open for 12% -> 4% of each run, Pallas kernels for 0% -> 4%
where the time goes in v1:
time: 102 us; the launch traced here: 100 us
  blocking collectives  48.4 us (47%)
  waiting for transfers between devices  23.9 us (23%)
  Pallas kernels  14.4 us (14%)
  other arithmetic  5.38 us (5%)
  starting transfers between devices  3.92 us (4%)
  local copies, waits for them, and re-layouts  3.67 us (4%)
    all_to_all x1, blocking collectives, body(): lax.all_to_all(sent.reshape(replicas, rows // replicas, LANES), 'rep', sp...  26.3 us
    ppermute x3, waiting for transfers between devices, body(): terms.append(lax.ppermute(both, 'fsdp', hop(n)))  23.9 us
    all_to_all x1, blocking collectives, body(): lax.all_to_all(mixed, 'rep', split_axis=0, concat_axis=0, tiled=True)  22.2 us
    pallas_call x2, Pallas kernels, unpack_pieces(): pl.pallas_call(kernel, in_specs=[pl.BlockSpec(memory_space=pltpu.SMEM), p...  8.11 us
    pallas_call x1, Pallas kernels, transform_step(): pl.pallas_call(kernel, grid=(rows // step,), in_specs=[block] * (len(term...  5.97 us
    unnamed x14, local copies, waits for them, and re-layouts  3.42 us
    ppermute x3, starting transfers between devices, body(): terms.append(lax.ppermute(both, 'fsdp', hop(n)))  2.82 us
    convert_element_type x3, other arithmetic, body(): both = (mine[i].astype(F32) + given[i].astype(F32)).astype(BF16)  2.8 us
  transfers between devices with their start and end apart: 7, of which 2 were waited for; matrix products, arithmetic and copies ran while one was open for 4% of the time, Pallas kernels for 4%

profile of v1, /device:TPU:24, one launch (start us, length us, event | category | flops | bytes accessed | tf_op | source)
XLA Modules:
  0.0 100.5 jit_solution(10360462076687054050)
XLA Ops:
  0.6 0.7 broadcast_add_fusion
  1.3 3.4 %copy-done = bf16[1,1,2097152]{2,1,0:T(2,128)(2,1)S(1)} copy-done((bf16[1,1,2097152]{2,1,0:T(2,128)(2,1)S(1)}, bf16[1,1,2097152]{2,1,0:T(2,128)(2,1)}, u32[]{:S(2)}) %copy-start) | copy-done | bytes 4194328
  4.7 4.4 %shard_map.87 = (bf16[2048,128]{1,0:T(8,128)(2,1)S(1)}, bf16[2048,128]{1,0:T(8,128)(2,1)S(1)}, bf16[2048,128]{1,0:T(8,128)(2,1)S(1)}, bf16[2048,128]{1,0:T(8,128)(2,1)}) custom-call(s32[4]{0:T(128)S(1)} %get-tuple-element.22.order_ref, bf16[1,1,2097152]{2,1,0:T(2,128)(2,1)S(1)} %copy-done), custom_call_target="tpu_custom_call" | custom-call | bytes 6291456 | tf_op jit(solution)/shard_map/pallas_call | solution.py:61
  9.1 0.1 collective-permute-start.1
  9.2 0.5 collective-permute-start.3
  9.7 0.1 collective-permute-start.5
  9.8 0.4 collective-permute-start
  10.3 3.7 %shard_map.86 = (bf16[2048,128]{1,0:T(8,128)(2,1)S(1)}, bf16[2048,128]{1,0:T(8,128)(2,1)S(1)}, bf16[2048,128]{1,0:T(8,128)(2,1)S(1)}, bf16[2048,128]{1,0:T(8,128)(2,1)S(1)}) custom-call(s32[4]{0:T(128)S(1)} %broadcast_add_fusion.1.order_ref, bf16[1,1,2097152]{2,1,0:T(2,128)(2,1)S(1)} %copy-done.1), custom_call_target="tpu_custom_call" | custom-call | bytes 6291456 | tf_op jit(solution)/shard_map/pallas_call | solution.py:61
  13.9 0.0 copy-start.6
  14.0 0.0 copy-start.5
  14.0 0.0 copy-start.2
  14.0 0.0 copy-start.3
  14.0 0.0 copy-start.4
  14.0 0.0 collective-permute-done.1
  14.0 0.9 add_convert_fusion.2
  14.9 2.0 %collective-permute-start.2 = (bf16[2048,128]{1,0:T(8,128)(2,1)}, bf16[2048,128]{1,0:T(8,128)(2,1)S(1)}, u32[]{:S(2)}, u32[]{:S(2)}) collective-permute-start(bf16[2048,128]{1,0:T(8,128)(2,1)} %add_convert_fusion.2), channel_id=1, source_target_pairs={{0,2},{1,3},{2,4},{3,5},{4,6},{5,7},{6,0},{7,1},{8,10},{9,11},{10,... | collective-permute-start | bytes 1572872 | tf_op jit(solution)/shard_map/ppermute | solution.py:153
  16.9 0.0 collective-permute-done.3
  16.9 0.9 add_convert_fusion.1
  17.8 0.9 collective-permute-start.4
  18.7 0.0 collective-permute-done.5
  18.7 0.9 add_convert_fusion
  19.6 0.0 collective-permute-start.6
  19.7 0.8 fusion.1
  20.5 0.1 copy.10
  20.7 19.3 %collective-permute-done.2.refs_2_ = bf16[2048,128]{1,0:T(8,128)(2,1)S(1)} collective-permute-done((bf16[2048,128]{1,0:T(8,128)(2,1)}, bf16[2048,128]{1,0:T(8,128)(2,1)S(1)}, u32[]{:S(2)}, u32[]{:S(2)}) %collective-permute-start.2) | collective-permute-done | bytes 524320 | tf_op jit(solution)/shard_map/ppermute | solution.py:153
  39.9 4.6 %collective-permute-done.6.refs_4_ = bf16[2048,128]{1,0:T(8,128)(2,1)} collective-permute-done((bf16[2048,128]{1,0:T(8,128)(2,1)}, bf16[2048,128]{1,0:T(8,128)(2,1)}, u32[]{:S(2)}, u32[]{:S(2)}) %collective-permute-start.6) | collective-permute-done | bytes 524320 | tf_op jit(solution)/shard_map/ppermute | solution.py:153
  44.5 0.1 broadcast_in_dim.2
  44.7 6.0 %shard_map.88 = (bf16[2048,128]{1,0:T(8,128)(2,1)S(1)}, f32[2048,128]{1,0:T(8,128)}) custom-call(bf16[2048,128]{1,0:T(8,128)(2,1)S(1)} %get-tuple-element.12.refs_0_, bf16[2048,128]{1,0:T(8,128)(2,1)S(1)} %collective-permute-done.refs_1_, bf16[2048,128]{1,0:T(8,128)(2,1)S(1)} %collective-permute-done.2.refs_2_, ...), custom_call_target="tpu_custom_call" | custom-call | flops 805306368 | bytes 6291456 | tf_op jit(solution)/shard_map/pallas_call | solution.py:95
  50.7 26.3 %all_to_all.10.pieces_ref = bf16[32,64,128]{2,1,0:T(8,128)(2,1)S(1)} all-to-all(bf16[32,64,128]{2,1,0:T(8,128)(2,1)S(1)} %bitcast.10), channel_id=1, replica_groups=mesh['rep'=32,'fsdp'=8] {'rep'}, dimensions={0} | all-to-all | bytes 1048576 | tf_op jit(solution)/shard_map/all_to_all | solution.py:168
  76.9 0.3 shard_map.89
  77.2 22.2 %all_to_all.11 = bf16[32,64,128]{2,1,0:T(8,128)(2,1)S(1)} all-to-all(bf16[32,64,128]{2,1,0:T(8,128)(2,1)S(1)} %shard_map.89), channel_id=1, replica_groups=mesh['rep'=32,'fsdp'=8] {'rep'}, dimensions={0} | all-to-all | bytes 1048576 | tf_op jit(solution)/shard_map/all_to_all | solution.py:172
  99.4 1.0 %convert.2 = f32[262144]{0:T(1024)} convert(bf16[262144]{0:T(1024)(128)(2,1)S(1)} %bitcast.11) | non-fusion elementwise | flops 262144 | bytes 1572864 | tf_op jit(solution)/shard_map/reshape | solution.py:173
  (13 shorter events, 0.1 us)
Async XLA Ops:
  1.3 3.4 %copy-start = (bf16[1,1,2097152]{2,1,0:T(2,128)(2,1)S(1)}, bf16[1,1,2097152]{2,1,0:T(2,128)(2,1)}, u32[]{:S(2)}) copy-start(bf16[1,1,2097152]{2,1,0:T(2,128)(2,1)} %raw_ref.3) | copy-start | bytes 12582916
  4.7 5.5 %copy-start.1 = (bf16[1,1,2097152]{2,1,0:T(2,128)(2,1)S(1)}, bf16[1,1,2097152]{2,1,0:T(2,128)(2,1)}, u32[]{:S(2)}) copy-start(bf16[1,1,2097152]{2,1,0:T(2,128)(2,1)} %raw_ref.3) | copy-start | bytes 12582916
  9.1 4.9 %collective-permute-start.1 = (bf16[2048,128]{1,0:T(8,128)(2,1)S(1)}, bf16[2048,128]{1,0:T(8,128)(2,1)S(1)}, u32[]{:S(2)}, u32[]{:S(2)}) collective-permute-start(bf16[2048,128]{1,0:T(8,128)(2,1)S(1)} %get-tuple-element.15), channel_id=1, source_target_pairs={{0,1},{1,0},{2,3},{3,2},{4,5},{5,4},{6,7},{7,6},{8,9},{9,8},{10,11... | collective-permute-start | bytes 1572872 | tf_op jit(solution)/shard_map/ppermute | solution.py:145
  9.2 7.7 %collective-permute-start.3 = (bf16[2048,128]{1,0:T(8,128)(2,1)S(1)}, bf16[2048,128]{1,0:T(8,128)(2,1)S(1)}, u32[]{:S(2)}, u32[]{:S(2)}) collective-permute-start(bf16[2048,128]{1,0:T(8,128)(2,1)S(1)} %get-tuple-element.17), channel_id=1, source_target_pairs={{0,1},{1,0},{2,3},{3,2},{4,5},{5,4},{6,7},{7,6},{8,9},{9,8},{10,11... | collective-permute-start | bytes 1572872 | tf_op jit(solution)/shard_map/ppermute | solution.py:145
  9.7 9.0 %collective-permute-start.5 = (bf16[2048,128]{1,0:T(8,128)(2,1)S(1)}, bf16[2048,128]{1,0:T(8,128)(2,1)S(1)}, u32[]{:S(2)}, u32[]{:S(2)}) collective-permute-start(bf16[2048,128]{1,0:T(8,128)(2,1)S(1)} %get-tuple-element.19), channel_id=1, source_target_pairs={{0,1},{1,0},{2,3},{3,2},{4,5},{5,4},{6,7},{7,6},{8,9},{9,8},{10,11... | collective-permute-start | bytes 1572872 | tf_op jit(solution)/shard_map/ppermute | solution.py:145
  9.8 10.8 %collective-permute-start = (bf16[2048,128]{1,0:T(8,128)(2,1)}, bf16[2048,128]{1,0:T(8,128)(2,1)S(1)}, u32[]{:S(2)}, u32[]{:S(2)}) collective-permute-start(bf16[2048,128]{1,0:T(8,128)(2,1)} %get-tuple-element.13), channel_id=1, source_target_pairs={{0,1},{1,0},{2,3},{3,2},{4,5},{5,4},{6,7},{7,6},{8,9},{9,8},{10,11... | collective-permute-start | bytes 1572872 | tf_op jit(solution)/shard_map/ppermute | solution.py:145
  13.9 5.7 %copy-start.6 = (s32[1,512]{1,0:T(1,128)S(1)}, s32[1,512]{1,0:T(1,128)}, u32[]{:S(2)}) copy-start(s32[1,512]{1,0:T(1,128)} %param.10) | copy-start | bytes 6148
  14.0 5.7 %copy-start.5 = (s32[1,512,32]{1,2,0:T(8,128)S(1)}, s32[1,512,32]{1,2,0:T(8,128)}, u32[]{:S(2)}) copy-start(s32[1,512,32]{1,2,0:T(8,128)} %param.9) | copy-start | bytes 196612
  14.0 30.7 %copy-start.2 = (f32[1,262144]{1,0:T(1,128)S(1)}, f32[1,262144]{1,0:T(1,128)}, u32[]{:S(2)}) copy-start(f32[1,262144]{1,0:T(1,128)} %param.8) | copy-start | bytes 3145732
  14.0 30.7 %copy-start.3 = (f32[128,128]{1,0:T(8,128)S(1)}, f32[128,128]{1,0:T(8,128)}, u32[]{:S(2)}) copy-start(f32[128,128]{1,0:T(8,128)} %constant.54.clone.refs_8_.inv_ref) | copy-start | bytes 196612
  14.0 30.7 %copy-start.4 = (f32[128,128]{1,0:T(8,128)S(1)}, f32[128,128]{1,0:T(8,128)}, u32[]{:S(2)}) copy-start(f32[128,128]{1,0:T(8,128)} %constant.53.clone.refs_7_) | copy-start | bytes 196612
  14.9 25.0 %collective-permute-start.2 = (bf16[2048,128]{1,0:T(8,128)(2,1)}, bf16[2048,128]{1,0:T(8,128)(2,1)S(1)}, u32[]{:S(2)}, u32[]{:S(2)}) collective-permute-start(bf16[2048,128]{1,0:T(8,128)(2,1)} %add_convert_fusion.2), channel_id=1, source_target_pairs={{0,2},{1,3},{2,4},{3,5},{4,6},{5,7},{6,0},{7,1},{8,10},{9,11},{10,... | collective-permute-start | bytes 1572872 | tf_op jit(solution)/shard_map/ppermute | solution.py:153
  17.8 22.1 %collective-permute-start.4 = (bf16[2048,128]{1,0:T(8,128)(2,1)}, bf16[2048,128]{1,0:T(8,128)(2,1)S(1)}, u32[]{:S(2)}, u32[]{:S(2)}) collective-permute-start(bf16[2048,128]{1,0:T(8,128)(2,1)} %add_convert_fusion.1), channel_id=1, source_target_pairs={{0,4},{1,5},{2,6},{3,7},{4,0},{5,1},{6,2},{7,3},{8,12},{9,13},{10,... | collective-permute-start | bytes 1572872 | tf_op jit(solution)/shard_map/ppermute | solution.py:153
  19.6 24.9 %collective-permute-start.6 = (bf16[2048,128]{1,0:T(8,128)(2,1)}, bf16[2048,128]{1,0:T(8,128)(2,1)}, u32[]{:S(2)}, u32[]{:S(2)}) collective-permute-start(bf16[2048,128]{1,0:T(8,128)(2,1)} %add_convert_fusion), channel_id=1, source_target_pairs={{0,6},{1,7},{2,0},{3,1},{4,2},{5,3},{6,4},{7,5},{8,14},{9,15},{10,... | collective-permute-start | bytes 1572872 | tf_op jit(solution)/shard_map/ppermute | solution.py:153

commit v2 on v0

v2 whole, which is shorter than its diff:
```python
import math

import jax
import jax.numpy as jnp
import numpy as np
from jax import lax
from jax.experimental import pallas as pl
from jax.experimental.pallas import tpu as pltpu
from jax.sharding import PartitionSpec as P

SEG = 64
GROUP = 8
KMAX = 32
LANES = 128
CORES = 2
PIECES = 8
VMEM_LIMIT = 20 << 20

BF16 = jnp.bfloat16
F32 = jnp.float32
VMEM = pl.BlockSpec(memory_space=pltpu.VMEM)


def paired_table():
    freq = np.arange(SEG, dtype=np.float64)[:, None]
    point = np.arange(SEG, dtype=np.float64)[None, :]
    scale = np.where(freq == 0.0, math.sqrt(1.0 / SEG), math.sqrt(2.0 / SEG))
    table = scale * np.cos(math.pi * (2.0 * point + 1.0) * freq / (2.0 * SEG))
    paired = np.kron(np.eye(2), table).astype(np.float32)
    high = paired.astype(BF16)
    low = (paired - high.astype(np.float32)).astype(BF16)
    return high, low


def forward_table():
    high, low = paired_table()
    return np.block([[high.T, low.T], [high.T, np.zeros_like(low)]]).astype(BF16)


def inverse_table():
    high, low = paired_table()
    return np.block([[high, low], [high, np.zeros_like(low)]]).astype(BF16)


def split(x):
    high = x.astype(BF16)
    low = (x - high.astype(F32)).astype(BF16)
    return jnp.concatenate([high, low], axis=1)


def product(x, table):
    out = jnp.dot(x, table, preferred_element_type=F32)
    return out[:, :LANES] + out[:, LANES:]


def unpack(raw, wanted):
    count = len(wanted)
    size = raw.shape[-1] // PIECES
    rows = size // LANES
    cuts = 2
    cut = size // cuts
    lines = cut // LANES
    step = min(lines, 128)

    def kernel(raw_ref, *refs):
        outs, (held, sems) = refs[:count], refs[count:]
        me = lax.axis_index("fsdp")
        chip, core = me // CORES, lax.rem(me, CORES)

        def fetch(i, j):
            n, other = wanted[i]
            lane = lax.rem(core + other, CORES)
            to = (chip, chip + 1 - 2 * lax.rem(chip, 2), lax.rem(chip + 2, 4), 3 - chip)[n]
            piece = to * CORES + lane
            at = pl.multiple_of(piece * size + j * cut, cut)
            return pltpu.make_async_copy(
                raw_ref.at[:, :, pl.ds(at, cut)], held.at[i * cuts + j], sems.at[i * cuts + j]
            )

        for i in range(count):
            for j in range(cuts):
                fetch(i, j).start()
        for i in range(count):
            for j in range(cuts):
                fetch(i, j).wait()
                for k in range(lines // step):
                    some = held[i * cuts + j, 0, :, pl.ds(k * step * LANES, step * LANES)]
                    outs[i][pl.ds(j * lines + k * step, step), :] = some.reshape(step, LANES)

    return pl.pallas_call(
        kernel,
        in_specs=[pl.BlockSpec(memory_space=pltpu.HBM)],
        out_specs=[VMEM] * count,
        out_shape=[jax.ShapeDtypeStruct((rows, LANES), BF16)] * count,
        scratch_shapes=[
            pltpu.VMEM((count * cuts, 1, 1, cut), BF16),
            pltpu.SemaphoreType.DMA((count * cuts,)),
        ],
        compiler_params=pltpu.CompilerParams(vmem_limit_bytes=VMEM_LIMIT),
        cost_estimate=pl.CostEstimate(flops=0, bytes_accessed=count * size * 6, transcendentals=0),
    )(raw)


def local_kernel(kernel, shapes, *args):
    return pl.pallas_call(
        kernel,
        in_specs=[VMEM] * len(args),
        out_specs=[VMEM] * len(shapes),
        out_shape=[jax.ShapeDtypeStruct(s, t) for s, t in shapes],
        compiler_params=pltpu.CompilerParams(vmem_limit_bytes=VMEM_LIMIT),
        cost_estimate=pl.CostEstimate(
            flops=0, bytes_accessed=sum(a.size * a.dtype.itemsize for a in args), transcendentals=0
        ),
    )(*args)


def far_kernel(mine_ref, given_ref, low_ref, high_ref):
    half = low_ref.shape[0]
    for at, out in ((0, low_ref), (half, high_ref)):
        some = pl.ds(at, half)
        out[...] = (mine_ref[some, :].astype(F32) + given_ref[some, :].astype(F32)).astype(BF16)


def near_kernel(mine1_ref, given1_ref, mine3_ref, given3_ref, near1_ref, near3_ref, sum1_ref, sum3_ref):
    half = near1_ref.shape[0]
    low, high = pl.ds(0, half), pl.ds(half, half)
    near1_ref[...] = (mine1_ref[low, :].astype(F32) + given1_ref[low, :].astype(F32)).astype(BF16)
    near3_ref[...] = (mine3_ref[high, :].astype(F32) + given3_ref[high, :].astype(F32)).astype(BF16)
    sum1_ref[...] = mine1_ref[high, :].astype(F32) + given1_ref[high, :].astype(F32)
    sum3_ref[...] = mine3_ref[low, :].astype(F32) + given3_ref[low, :].astype(F32)


def last_kernel(sum_ref, far_ref, out_ref):
    out_ref[...] = (sum_ref[...] + far_ref[...].astype(F32)).astype(BF16)


def base_kernel(mom_ref, mine_ref, given_ref, low_ref, high_ref, hot_ref, fwd_ref, inv_ref, out_ref, mask_ref):
    half = low_ref.shape[0]
    for at, part in ((0, low_ref), (half, high_ref)):
        some = pl.ds(at, half)
        out_ref[some, :] = (
            0.999 * mom_ref[some, :]
            + mine_ref[some, :].astype(F32)
            + given_ref[some, :].astype(F32)
            + part[...].astype(F32)
        )
    blocks = hot_ref.shape[0]
    hot = hot_ref[...].astype(F32)
    for q in range(GROUP // 2):
        mask_ref[pl.ds(q, blocks, stride=GROUP // 2), :] = hot


def guess_kernel(base_ref, fwd_ref, coeff_ref):
    rows = base_ref.shape[0]
    step = min(rows, 256)
    for k in range(rows // step):
        some = pl.ds(k * step, step)
        coeff_ref[some, :] = product(split(base_ref[some, :]), fwd_ref[...])


def keep_kernel(coeff_ref, low_ref, high_ref, mask_ref, fwd_ref, sent_ref):
    half = low_ref.shape[0]
    step = min(half, 256)
    for at, part in ((0, low_ref), (half, high_ref)):
        for k in range(half // step):
            some = pl.ds(at + k * step, step)
            coeff = coeff_ref[some, :] + product(part[pl.ds(k * step, step), :], fwd_ref[:LANES, :])
            sent_ref[some, :] = jnp.where(mask_ref[some, :] > 0.5, coeff, 0.0).astype(BF16)


def remove_kernel(sent_ref, base_ref, low_ref, high_ref, inv_ref, new_ref):
    half = low_ref.shape[0]
    step = min(half, 256)
    for at, part in ((0, low_ref), (half, high_ref)):
        for k in range(half // step):
            some = pl.ds(at + k * step, step)
            moment = base_ref[some, :] + part[pl.ds(k * step, step), :].astype(F32)
            new_ref[some, :] = moment - product(sent_ref[some, :], inv_ref[:LANES, :])


def combine_kernel(factor, pieces_ref, inv_ref, out_ref):
    total = jnp.sum(pieces_ref[...].astype(F32), axis=0)
    back = product(split(total), inv_ref[...]) * factor
    out_ref[...] = jnp.broadcast_to(back.astype(BF16)[None], out_ref.shape)


def spread_kernel(zs, *refs):
    planes, out_ref = refs[:-1], refs[-1]
    count = planes[0].shape[0]
    x = lax.axis_index("rep") // zs
    order = (x, x + 1 - 2 * lax.rem(x, 2), lax.rem(x + 2, 4), 3 - x)
    for n, ref in enumerate(planes):
        out_ref[pl.ds(pl.multiple_of(order[n] * count, count), count), :] = ref[...].astype(F32)


def body(grad_parts, momentum, bands, counts):
    replicas = lax.axis_size("rep")
    holders = lax.axis_size("fsdp")
    forward, inverse = jnp.asarray(forward_table()), jnp.asarray(inverse_table())

    blocks = momentum.size // (GROUP * SEG)
    rows = momentum.size // LANES
    half = rows // 2

    freqs = jnp.arange(SEG, dtype=jnp.int32)
    slots = jnp.arange(KMAX, dtype=jnp.int32)
    lists = bands.reshape(blocks, KMAX)
    live = counts.reshape(blocks)
    hot = jnp.any(
        (lists[:, :, None] == freqs[None, None, :]) & (slots[None, :, None] < live[:, None, None]),
        axis=1,
    ).astype(BF16)
    hot = jnp.concatenate([hot, hot], axis=1)

    whole, part = (rows, LANES), (half, LANES)

    def over_cores(x):
        return lax.ppermute(x, "fsdp", [(f, f ^ 1) for f in range(holders)])

    def trade(x, n):
        return lax.ppermute(x, "fsdp", [(f, f ^ (CORES * n)) for f in range(holders)])

    (theirs2,) = unpack(grad_parts, ((2, 1),))
    given2 = over_cores(theirs2)
    mine2, theirs1, theirs3, mine1, mine3, theirs0, mine0 = unpack(
        grad_parts, ((2, 0), (1, 1), (3, 1), (1, 0), (3, 0), (0, 1), (0, 0))
    )
    given1, given3 = over_cores(theirs1), over_cores(theirs3)
    far1, far3 = local_kernel(far_kernel, [(part, BF16)] * 2, mine2, given2)
    far1, far3 = trade(far1, 1), trade(far3, 3)
    given0 = over_cores(theirs0)
    near1, near3, sum1, sum3 = local_kernel(
        near_kernel, [(part, BF16)] * 2 + [(part, F32)] * 2, mine1, given1, mine3, given3
    )
    near_low, near_high = trade(near1, 1), trade(near3, 3)
    (last3,) = local_kernel(last_kernel, [(part, BF16)], sum3, far1)
    last_low = trade(last3, 3)
    (last1,) = local_kernel(last_kernel, [(part, BF16)], sum1, far3)
    last_high = trade(last1, 1)

    base, mask = local_kernel(
        base_kernel,
        [(whole, F32)] * 2,
        momentum.reshape(whole),
        mine0,
        given0,
        near_low,
        near_high,
        hot,
        forward,
        inverse,
    )
    (coeff,) = local_kernel(guess_kernel, [(whole, F32)], base, forward)
    (sent,) = local_kernel(keep_kernel, [(whole, BF16)], coeff, last_low, last_high, mask, forward)
    (new,) = local_kernel(remove_kernel, [(whole, F32)], sent, base, last_low, last_high, inverse)

    pieces = lax.all_to_all(
        sent.reshape(replicas, rows // replicas, LANES), "rep", split_axis=0, concat_axis=0, tiled=True
    )
    xs = 4
    zs = replicas // xs
    (mixed,) = local_kernel(
        lambda *refs: combine_kernel(1.0 / math.sqrt(replicas), *refs),
        [((zs,) + pieces.shape[1:], BF16)],
        pieces,
        inverse,
    )
    lines = [[zs * x + z for z in range(zs)] for x in range(xs)]
    plane = lax.all_to_all(
        mixed, "rep", split_axis=0, concat_axis=0, axis_index_groups=lines, tiled=True
    ).reshape(rows // xs, LANES)

    def across(n):
        return lax.ppermute(plane, "rep", [(r, r ^ (zs * n)) for r in range(replicas)])

    planes = [plane] + [across(n) for n in (1, 2, 3)]
    (update,) = local_kernel(lambda *refs: spread_kernel(zs, *refs), [(whole, F32)], *planes)
    return (new.reshape(momentum.shape), update.reshape(-1))


def solution(mesh):
    placed = (P("rep", "fsdp", None), P("rep", "fsdp"), P("rep", "fsdp", None), P("rep", "fsdp"))
    return jax.shard_map(
        body, mesh=mesh, in_specs=placed, out_specs=(P("rep", "fsdp"), P("fsdp")), check_vma=False
    )
```

time: 459 us -> 79.8 us (0.17)
  matrix products: 135 us -> 0 us
  waiting for transfers between devices: 144 us -> 13.5 us
  local copies, waits for them, and re-layouts: 113 us -> 3.58 us
  other arithmetic: 44.4 us -> 0.99 us
  blocking collectives: 0 us -> 40.7 us
  between operations: 14.2 us -> 0.78 us
  Pallas kernels: 0 us -> 8.46 us
  starting transfers between devices: 6.82 us -> 11.6 us
    dot_general x13 -> x0, matrix products: 135 us -> none  [the longest x8 111 us: add_group(): jnp.einsum('rcgk,rckf->cgf', vals, hot, preferred_element_type=jnp.float32)]
    all_gather x2 -> x0, waiting for transfers between devices: 98.2 us -> none  [the longest x1 98.2 us: body(): lax.all_gather(values.reshape(blocks, GROUP * KMAX), 'rep', axis=0, tiled...]
    dynamic_slice x32 -> x0, local copies, waits for them, and re-layouts: 70.9 us -> none  [the longest x16 67.5 us: add_group(): vals = lax.dynamic_index_in_dim(vals_all, turn, 0, keepdims=False)]
    all_to_all x1 -> x0, waiting for transfers between devices: 44.8 us -> none  [body(): lax.all_to_all(pieces, 'fsdp', split_axis=0, concat_axis=0, tiled=True)]
    all_to_all x0 -> x2, blocking collectives: none -> 40.7 us  [the longest x1 27.9 us: body(): lax.all_to_all(sent.reshape(replicas, rows // replicas, LANES), 'rep', sp...]
    all_to_all x1 -> x0, other arithmetic: 27.1 us -> none  [body(): lax.all_to_all(pieces, 'fsdp', split_axis=0, concat_axis=0, tiled=True)]
    reshape x5 -> x0, local copies, waits for them, and re-layouts: 22.5 us -> none  [the longest x1 14.5 us: body(): vals_all = piece_vals.reshape(turns, batch, blocks, GROUP, KMAX)]
    ppermute x0 -> x13, waiting for transfers between devices: none -> 13.5 us  [the longest x6 10.5 us: trade(): return lax.ppermute(x, 'fsdp', [(f, f ^ CORES * n) for f in range(holders)])]
  transfers between devices with their start and end apart: 3 -> 13, of which waited for: 2 -> 7; matrix products, arithmetic and copies ran while one was open for 12% -> 1% of each run, Pallas kernels for 0% -> 8%
where the time goes in v2:
time: 79.8 us; the launch traced here: 79.6 us
  blocking collectives  40.7 us (51%)
  waiting for transfers between devices  13.5 us (17%)
  starting transfers between devices  11.6 us (15%)
  Pallas kernels  8.46 us (11%)
  local copies, waits for them, and re-layouts  3.58 us (4%)
  other arithmetic  0.99 us (1%)
    all_to_all x1, blocking collectives, body(): lax.all_to_all(sent.reshape(replicas, rows // replicas, LANES), 'rep', sp...  27.9 us
    all_to_all x1, blocking collectives, body(): lax.all_to_all(mixed, 'rep', split_axis=0, concat_axis=0, axis_index_grou...  12.8 us
    ppermute x6, waiting for transfers between devices, trade(): return lax.ppermute(x, 'fsdp', [(f, f ^ CORES * n) for f in range(holders)])  10.5 us
    ppermute x6, starting transfers between devices, trade(): return lax.ppermute(x, 'fsdp', [(f, f ^ CORES * n) for f in range(holders)])  6.56 us
    pallas_call x10, Pallas kernels, local_kernel(): pl.pallas_call(kernel, in_specs=[VMEM] * len(args), out_specs=[VMEM] * le...  6.36 us
    ppermute x3, starting transfers between devices, across(): lax.ppermute(plane, 'rep', [(r, r ^ zs * n) for r in range(replicas)])  4.09 us
    unnamed x12, local copies, waits for them, and re-layouts  3.41 us
    ppermute x3, waiting for transfers between devices, across(): lax.ppermute(plane, 'rep', [(r, r ^ zs * n) for r in range(replicas)])  2.96 us
  transfers between devices with their start and end apart: 13, of which 7 were waited for; matrix products, arithmetic and copies ran while one was open for 1% of the time, Pallas kernels for 8%

profile of v2, /device:TPU:24, one launch (start us, length us, event | category | flops | bytes accessed | tf_op | source)
XLA Modules:
  0.0 79.6 jit_solution(3576364753824127232)
XLA Ops:
  0.6 3.4 %copy-done = bf16[1,1,2097152]{2,1,0:T(2,128)(2,1)S(1)} copy-done((bf16[1,1,2097152]{2,1,0:T(2,128)(2,1)S(1)}, bf16[1,1,2097152]{2,1,0:T(2,128)(2,1)}, u32[]{:S(2)}) %copy-start) | copy-done | bytes 4194328
  4.0 0.2 shard_map.81
  4.3 1.9 %shard_map.77 = (bf16[2048,128]{1,0:T(8,128)(2,1)S(1)}, bf16[2048,128]{1,0:T(8,128)(2,1)S(1)}, bf16[2048,128]{1,0:T(8,128)(2,1)S(1)}, bf16[2048,128]{1,0:T(8,128...) custom-call(bf16[1,1,2097152]{2,1,0:T(2,128)(2,1)S(1)} %copy-done), custom_call_target="tpu_custom_call" | custom-call | bytes 11010048 | tf_op jit(solution)/shard_map/pallas_call | solution.py:90
  6.3 0.6 collective-permute-start.1
  7.1 0.8 %collective-permute-start.6 = (bf16[1024,128]{1,0:T(8,128)(2,1)S(1)}, bf16[1024,128]{1,0:T(8,128)(2,1)S(1)}, u32[]{:S(2)}, u32[]{:S(2)}) collective-permute-start(bf16[1024,128]{1,0:T(8,128)(2,1)S(1)} %get-tuple-element.28), channel_id=1, source_target_pairs={{0,2},{1,3},{2,0},{3,1},{4,6},{5,7},{6,4},{7,5},{8,10},{9,11},{10,... | collective-permute-start | bytes 786440 | tf_op jit(solution)/shard_map/ppermute | solution.py:221
  7.9 1.3 %collective-permute-start.8 = (bf16[1024,128]{1,0:T(8,128)(2,1)S(1)}, bf16[1024,128]{1,0:T(8,128)(2,1)S(1)}, u32[]{:S(2)}, u32[]{:S(2)}) collective-permute-start(bf16[1024,128]{1,0:T(8,128)(2,1)S(1)} %get-tuple-element.30), channel_id=1, source_target_pairs={{0,6},{1,7},{2,4},{3,5},{4,2},{5,3},{6,0},{7,1},{8,14},{9,15},{10,... | collective-permute-start | bytes 786440 | tf_op jit(solution)/shard_map/ppermute | solution.py:221
  9.4 0.9 %shard_map.78 = (bf16[1024,128]{1,0:T(8,128)(2,1)}, bf16[1024,128]{1,0:T(8,128)(2,1)}, f32[1024,128]{1,0:T(8,128)S(1)}, f32[1024,128]{1,0:T(8,128)S(1)}) custom-call(bf16[2048,128]{1,0:T(8,128)(2,1)S(1)} %get-tuple-element.19.mine1_ref, bf16[2048,128]{1,0:T(8,128)(2,1)S(1)} %collective-permute-done.1.given1_ref, ...), custom_call_target="tpu_custom_call" | custom-call | bytes 2097152 | tf_op jit(solution)/shard_map/pallas_call | solution.py:105
  10.3 1.2 %collective-permute-start.3 = (bf16[1024,128]{1,0:T(8,128)(2,1)}, bf16[1024,128]{1,0:T(8,128)(2,1)S(1)}, u32[]{:S(2)}, u32[]{:S(2)}) collective-permute-start(bf16[1024,128]{1,0:T(8,128)(2,1)} %get-tuple-element.23), channel_id=1, source_target_pairs={{0,2},{1,3},{2,0},{3,1},{4,6},{5,7},{6,4},{7,5},{8,10},{9,11},{10,... | collective-permute-start | bytes 786440 | tf_op jit(solution)/shard_map/ppermute | solution.py:221
  11.5 1.3 %collective-permute-start.4 = (bf16[1024,128]{1,0:T(8,128)(2,1)}, bf16[1024,128]{1,0:T(8,128)(2,1)S(1)}, u32[]{:S(2)}, u32[]{:S(2)}) collective-permute-start(bf16[1024,128]{1,0:T(8,128)(2,1)} %get-tuple-element.24), channel_id=1, source_target_pairs={{0,6},{1,7},{2,4},{3,5},{4,2},{5,3},{6,0},{7,1},{8,14},{9,15},{10,... | collective-permute-start | bytes 786440 | tf_op jit(solution)/shard_map/ppermute | solution.py:221
  12.8 3.5 %collective-permute-done.6.far_ref = bf16[1024,128]{1,0:T(8,128)(2,1)S(1)} collective-permute-done((bf16[1024,128]{1,0:T(8,128)(2,1)S(1)}, bf16[1024,128]{1,0:T(8,128)(2,1)S(1)}, u32[]{:S(2)}, u32[]{:S(2)}) %collective-permute-start.6) | collective-permute-done | bytes 262176 | tf_op jit(solution)/shard_map/ppermute | solution.py:221
  16.3 0.7 shard_map.83
  17.0 2.0 %collective-permute-start.7 = (bf16[1024,128]{1,0:T(8,128)(2,1)}, bf16[1024,128]{1,0:T(8,128)(2,1)S(1)}, u32[]{:S(2)}, u32[]{:S(2)}) collective-permute-start(bf16[1024,128]{1,0:T(8,128)(2,1)} %shard_map.83), channel_id=1, source_target_pairs={{0,6},{1,7},{2,4},{3,5},{4,2},{5,3},{6,0},{7,1},{8,14},{9,15},{10,... | collective-permute-start | bytes 786440 | tf_op jit(solution)/shard_map/ppermute | solution.py:221
  19.0 0.8 shard_map.84
  19.7 0.8 %fusion.1 = pred[512,64]{0,1:T(8,128)(4,1)S(1)} fusion(s32[512,32]{0,1:T(8,128)S(1)} %bitcast.15, pred[512,32]{0,1:T(8,128)(4,1)S(1)} %iota_compare_fusion.1), kind=kLoop, calls=%fused_computation.2 | loop fusion | flops 3112960 | bytes 114688 | tf_op jit(solution)/shard_map/reduce_or | solution.py:209
  20.6 0.2 copy.9
  20.9 0.5 collective-permute-done.3.low_ref
  21.4 2.5 %collective-permute-done.4.high_ref = bf16[1024,128]{1,0:T(8,128)(2,1)S(1)} collective-permute-done((bf16[1024,128]{1,0:T(8,128)(2,1)}, bf16[1024,128]{1,0:T(8,128)(2,1)S(1)}, u32[]{:S(2)}, u32[]{:S(2)}) %collective-permute-start.4) | collective-permute-done | bytes 262176 | tf_op jit(solution)/shard_map/ppermute | solution.py:221
  23.9 0.3 shard_map.79
  24.2 0.5 shard_map.80.coeff_ref
  24.7 4.0 %collective-permute-done.7.low_ref = bf16[1024,128]{1,0:T(8,128)(2,1)S(1)} collective-permute-done((bf16[1024,128]{1,0:T(8,128)(2,1)}, bf16[1024,128]{1,0:T(8,128)(2,1)S(1)}, u32[]{:S(2)}, u32[]{:S(2)}) %collective-permute-start.7) | collective-permute-done | bytes 262176 | tf_op jit(solution)/shard_map/ppermute | solution.py:221
  28.7 0.4 shard_map.85.sent_ref
  29.1 27.9 %all_to_all.10.refs_0_ = bf16[32,64,128]{2,1,0:T(8,128)(2,1)S(1)} all-to-all(bf16[32,64,128]{2,1,0:T(8,128)(2,1)S(1)} %bitcast.7), channel_id=1, replica_groups=mesh['rep'=32,'fsdp'=8] {'rep'}, dimensions={0} | all-to-all | bytes 1048576 | tf_op jit(solution)/shard_map/all_to_all | solution.py:257
  57.1 0.2 shard_map.87
  57.3 12.8 %all_to_all.11 = bf16[8,64,128]{2,1,0:T(8,128)(2,1)S(1)} all-to-all(bf16[8,64,128]{2,1,0:T(8,128)(2,1)S(1)} %shard_map.87), channel_id=1, replica_groups={{0,8,16,24,32,40,48,56},{64,72,80,88,96,104,112,120},{128,136,144,152,1..., dimensions={0} | all-to-all | bytes 262144 | tf_op jit(solution)/shard_map/all_to_all | solution.py:269
  70.1 1.1 %collective-permute-start.12 = (bf16[512,128]{1,0:T(8,128)(2,1)S(1)}, bf16[512,128]{1,0:T(8,128)(2,1)S(1)}, u32[]{:S(2)}, u32[]{:S(2)}) collective-permute-start(bf16[512,128]{1,0:T(8,128)(2,1)S(1)} %bitcast.9), channel_id=1, source_target_pairs={{0,192},{8,200},{16,208},{24,216},{32,224},{40,232},{48,240},{56,2... | collective-permute-start | bytes 393224 | tf_op jit(solution)/shard_map/ppermute | solution.py:274
  71.2 1.5 %collective-permute-start.11 = (bf16[512,128]{1,0:T(8,128)(2,1)S(1)}, bf16[512,128]{1,0:T(8,128)(2,1)S(1)}, u32[]{:S(2)}, u32[]{:S(2)}) collective-permute-start(bf16[512,128]{1,0:T(8,128)(2,1)S(1)} %bitcast.10), channel_id=1, source_target_pairs={{0,128},{8,136},{16,144},{24,152},{32,160},{40,168},{48,176},{56,1... | collective-permute-start | bytes 393224 | tf_op jit(solution)/shard_map/ppermute | solution.py:274
  72.8 1.4 %collective-permute-start.10 = (bf16[512,128]{1,0:T(8,128)(2,1)S(1)}, bf16[512,128]{1,0:T(8,128)(2,1)S(1)}, u32[]{:S(2)}, u32[]{:S(2)}) collective-permute-start(bf16[512,128]{1,0:T(8,128)(2,1)S(1)} %bitcast.11), channel_id=1, source_target_pairs={{0,64},{8,72},{16,80},{24,88},{32,96},{40,104},{48,112},{56,120},{... | collective-permute-start | bytes 393224 | tf_op jit(solution)/shard_map/ppermute | solution.py:274
  74.2 1.4 %shard_map.86 = f32[2048,128]{1,0:T(8,128)} custom-call(bf16[2048,128]{1,0:T(8,128)(2,1)S(1)} %shard_map.85.sent_ref, f32[2048,128]{1,0:T(8,128)S(1)} %get-tuple-element.25.base_ref, bf16[1024,128]{1,0:T(8,128)(2,1)S(1)} %collective-permute-done.7.low_ref, bf16[1024,128]{1,0:T(8,128)(2,1)S(1)} %collective-permute-done.9.high_ref, bf16[256,256]{1,0:T(8,128)(2,1)S(1)} %copy-done.2), custom_call_target="tpu_custom_call" | custom-call | bytes 2228224 | tf_op jit(solution)/shard_map/pallas_call | solution.py:105
  75.6 0.7 collective-permute-done.12.refs_3_
  76.3 1.4 %collective-permute-done.11.refs_2_ = bf16[512,128]{1,0:T(8,128)(2,1)S(1)} collective-permute-done((bf16[512,128]{1,0:T(8,128)(2,1)S(1)}, bf16[512,128]{1,0:T(8,128)(2,1)S(1)}, u32[]{:S(2)}, u32[]{:S(2)}) %collective-permute-start.11) | collective-permute-done | bytes 131104 | tf_op jit(solution)/shard_map/ppermute | solution.py:274
  77.7 0.8 %collective-permute-done.10.refs_1_ = bf16[512,128]{1,0:T(8,128)(2,1)S(1)} collective-permute-done((bf16[512,128]{1,0:T(8,128)(2,1)S(1)}, bf16[512,128]{1,0:T(8,128)(2,1)S(1)}, u32[]{:S(2)}, u32[]{:S(2)}) %collective-permute-start.10) | collective-permute-done | bytes 131104 | tf_op jit(solution)/shard_map/ppermute | solution.py:274
  78.5 1.1 %shard_map.88 = f32[2048,128]{1,0:T(8,128)} custom-call(bf16[512,128]{1,0:T(8,128)(2,1)S(1)} %bitcast.12, bf16[512,128]{1,0:T(8,128)(2,1)S(1)} %collective-permute-done.10.refs_1_, bf16[512,128]{1,0:T(8,128)(2,1)S(1)} %collective-permute-done.11.refs_2_, bf16[512,128]{1,0:T(8,128)(2,1)S(1)} %collective-permute-done.12.refs_3_), custom_call_target="tpu_custom_call" | custom-call | bytes 524288 | tf_op jit(solution)/shard_map/pallas_call | solution.py:105
  (24 shorter events, 0.7 us)
Async XLA Ops:
  0.6 3.4 %copy-start = (bf16[1,1,2097152]{2,1,0:T(2,128)(2,1)S(1)}, bf16[1,1,2097152]{2,1,0:T(2,128)(2,1)}, u32[]{:S(2)}) copy-start(bf16[1,1,2097152]{2,1,0:T(2,128)(2,1)} %raw_ref.3) | copy-start | bytes 12582916
  4.2 5.2 %copy-start.5 = (s32[1,512]{1,0:T(1,128)S(1)}, s32[1,512]{1,0:T(1,128)}, u32[]{:S(2)}) copy-start(s32[1,512]{1,0:T(1,128)} %param.9) | copy-start | bytes 6148
  4.2 2.8 %collective-permute-start.5 = (bf16[2048,128]{1,0:T(8,128)(2,1)S(1)}, bf16[2048,128]{1,0:T(8,128)(2,1)S(1)}, u32[]{:S(2)}, u32[]{:S(2)}) collective-permute-start(bf16[2048,128]{1,0:T(8,128)(2,1)S(1)} %shard_map.81), channel_id=1, source_target_pairs={{0,1},{1,0},{2,3},{3,2},{4,5},{5,4},{6,7},{7,6},{8,9},{9,8},{10,11... | collective-permute-start | bytes 1572872 | tf_op jit(solution)/shard_map/ppermute | solution.py:218
  6.2 13.5 %copy-start.4 = (s32[1,512,32]{1,2,0:T(8,128)S(1)}, s32[1,512,32]{1,2,0:T(8,128)}, u32[]{:S(2)}) copy-start(s32[1,512,32]{1,2,0:T(8,128)} %param.8) | copy-start | bytes 196612
  6.3 17.6 %copy-start.1 = (bf16[256,256]{1,0:T(8,128)(2,1)S(1)}, bf16[256,256]{1,0:T(8,128)(2,1)}, u32[]{:S(2)}) copy-start(bf16[256,256]{1,0:T(8,128)(2,1)} %constant.6.clone.fwd_ref) | copy-start | bytes 393220
  6.3 17.6 %copy-start.2 = (bf16[256,256]{1,0:T(8,128)(2,1)S(1)}, bf16[256,256]{1,0:T(8,128)(2,1)}, u32[]{:S(2)}) copy-start(bf16[256,256]{1,0:T(8,128)(2,1)} %constant.7.clone.inv_ref.refs_1_) | copy-start | bytes 393220
  6.3 17.6 %copy-start.3 = (f32[1,262144]{1,0:T(1,128)S(1)}, f32[1,262144]{1,0:T(1,128)}, u32[]{:S(2)}) copy-start(f32[1,262144]{1,0:T(1,128)} %param.7) | copy-start | bytes 3145732
  6.3 3.1 %collective-permute-start.1 = (bf16[2048,128]{1,0:T(8,128)(2,1)S(1)}, bf16[2048,128]{1,0:T(8,128)(2,1)S(1)}, u32[]{:S(2)}, u32[]{:S(2)}) collective-permute-start(bf16[2048,128]{1,0:T(8,128)(2,1)S(1)} %get-tuple-element.20), channel_id=1, source_target_pairs={{0,1},{1,0},{2,3},{3,2},{4,5},{5,4},{6,7},{7,6},{8,9},{9,8},{10,11... | collective-permute-start | bytes 1572872 | tf_op jit(solution)/shard_map/ppermute | solution.py:218
  6.8 2.6 %collective-permute-start.2 = (bf16[2048,128]{1,0:T(8,128)(2,1)S(1)}, bf16[2048,128]{1,0:T(8,128)(2,1)S(1)}, u32[]{:S(2)}, u32[]{:S(2)}) collective-permute-start(bf16[2048,128]{1,0:T(8,128)(2,1)S(1)} %get-tuple-element.22), channel_id=1, source_target_pairs={{0,1},{1,0},{2,3},{3,2},{4,5},{5,4},{6,7},{7,6},{8,9},{9,8},{10,11... | collective-permute-start | bytes 1572872 | tf_op jit(solution)/shard_map/ppermute | solution.py:218
  7.1 9.2 %collective-permute-start.6 = (bf16[1024,128]{1,0:T(8,128)(2,1)S(1)}, bf16[1024,128]{1,0:T(8,128)(2,1)S(1)}, u32[]{:S(2)}, u32[]{:S(2)}) collective-permute-start(bf16[1024,128]{1,0:T(8,128)(2,1)S(1)} %get-tuple-element.28), channel_id=1, source_target_pairs={{0,2},{1,3},{2,0},{3,1},{4,6},{5,7},{6,4},{7,5},{8,10},{9,11},{10,... | collective-permute-start | bytes 786440 | tf_op jit(solution)/shard_map/ppermute | solution.py:221
  7.9 11.1 %collective-permute-start.8 = (bf16[1024,128]{1,0:T(8,128)(2,1)S(1)}, bf16[1024,128]{1,0:T(8,128)(2,1)S(1)}, u32[]{:S(2)}, u32[]{:S(2)}) collective-permute-start(bf16[1024,128]{1,0:T(8,128)(2,1)S(1)} %get-tuple-element.30), channel_id=1, source_target_pairs={{0,6},{1,7},{2,4},{3,5},{4,2},{5,3},{6,0},{7,1},{8,14},{9,15},{10,... | collective-permute-start | bytes 786440 | tf_op jit(solution)/shard_map/ppermute | solution.py:221
  9.2 11.7 %collective-permute-start = (bf16[2048,128]{1,0:T(8,128)(2,1)}, bf16[2048,128]{1,0:T(8,128)(2,1)S(1)}, u32[]{:S(2)}, u32[]{:S(2)}) collective-permute-start(bf16[2048,128]{1,0:T(8,128)(2,1)} %get-tuple-element.18), channel_id=1, source_target_pairs={{0,1},{1,0},{2,3},{3,2},{4,5},{5,4},{6,7},{7,6},{8,9},{9,8},{10,11... | collective-permute-start | bytes 1572872 | tf_op jit(solution)/shard_map/ppermute | solution.py:218
  10.3 11.1 %collective-permute-start.3 = (bf16[1024,128]{1,0:T(8,128)(2,1)}, bf16[1024,128]{1,0:T(8,128)(2,1)S(1)}, u32[]{:S(2)}, u32[]{:S(2)}) collective-permute-start(bf16[1024,128]{1,0:T(8,128)(2,1)} %get-tuple-element.23), channel_id=1, source_target_pairs={{0,2},{1,3},{2,0},{3,1},{4,6},{5,7},{6,4},{7,5},{8,10},{9,11},{10,... | collective-permute-start | bytes 786440 | tf_op jit(solution)/shard_map/ppermute | solution.py:221
  11.5 12.4 %collective-permute-start.4 = (bf16[1024,128]{1,0:T(8,128)(2,1)}, bf16[1024,128]{1,0:T(8,128)(2,1)S(1)}, u32[]{:S(2)}, u32[]{:S(2)}) collective-permute-start(bf16[1024,128]{1,0:T(8,128)(2,1)} %get-tuple-element.24), channel_id=1, source_target_pairs={{0,6},{1,7},{2,4},{3,5},{4,2},{5,3},{6,0},{7,1},{8,14},{9,15},{10,... | collective-permute-start | bytes 786440 | tf_op jit(solution)/shard_map/ppermute | solution.py:221
  17.0 11.7 %collective-permute-start.7 = (bf16[1024,128]{1,0:T(8,128)(2,1)}, bf16[1024,128]{1,0:T(8,128)(2,1)S(1)}, u32[]{:S(2)}, u32[]{:S(2)}) collective-permute-start(bf16[1024,128]{1,0:T(8,128)(2,1)} %shard_map.83), channel_id=1, source_target_pairs={{0,6},{1,7},{2,4},{3,5},{4,2},{5,3},{6,0},{7,1},{8,14},{9,15},{10,... | collective-permute-start | bytes 786440 | tf_op jit(solution)/shard_map/ppermute | solution.py:221
  19.7 9.0 %collective-permute-start.9 = (bf16[1024,128]{1,0:T(8,128)(2,1)}, bf16[1024,128]{1,0:T(8,128)(2,1)S(1)}, u32[]{:S(2)}, u32[]{:S(2)}) collective-permute-start(bf16[1024,128]{1,0:T(8,128)(2,1)} %shard_map.84), channel_id=1, source_target_pairs={{0,2},{1,3},{2,0},{3,1},{4,6},{5,7},{6,4},{7,5},{8,10},{9,11},{10,... | collective-permute-start | bytes 786440 | tf_op jit(solution)/shard_map/ppermute | solution.py:221
  70.1 6.2 %collective-permute-start.12 = (bf16[512,128]{1,0:T(8,128)(2,1)S(1)}, bf16[512,128]{1,0:T(8,128)(2,1)S(1)}, u32[]{:S(2)}, u32[]{:S(2)}) collective-permute-start(bf16[512,128]{1,0:T(8,128)(2,1)S(1)} %bitcast.9), channel_id=1, source_target_pairs={{0,192},{8,200},{16,208},{24,216},{32,224},{40,232},{48,240},{56,2... | collective-permute-start | bytes 393224 | tf_op jit(solution)/shard_map/ppermute | solution.py:274
  71.2 6.5 %collective-permute-start.11 = (bf16[512,128]{1,0:T(8,128)(2,1)S(1)}, bf16[512,128]{1,0:T(8,128)(2,1)S(1)}, u32[]{:S(2)}, u32[]{:S(2)}) collective-permute-start(bf16[512,128]{1,0:T(8,128)(2,1)S(1)} %bitcast.10), channel_id=1, source_target_pairs={{0,128},{8,136},{16,144},{24,152},{32,160},{40,168},{48,176},{56,1... | collective-permute-start | bytes 393224 | tf_op jit(solution)/shard_map/ppermute | solution.py:274
  72.8 5.8 %collective-permute-start.10 = (bf16[512,128]{1,0:T(8,128)(2,1)S(1)}, bf16[512,128]{1,0:T(8,128)(2,1)S(1)}, u32[]{:S(2)}, u32[]{:S(2)}) collective-permute-start(bf16[512,128]{1,0:T(8,128)(2,1)S(1)} %bitcast.11), channel_id=1, source_target_pairs={{0,64},{8,72},{16,80},{24,88},{32,96},{40,104},{48,112},{56,120},{... | collective-permute-start | bytes 393224 | tf_op jit(solution)/shard_map/ppermute | solution.py:274

commit v3 on v2

--- a/solution.py
+++ b/solution.py
@@ -15,6 +15,8 @@
 CORES = 2
 PIECES = 8
 VMEM_LIMIT = 20 << 20
+SUB = 8
+QUADS = GROUP // 2
 
 BF16 = jnp.bfloat16
 F32 = jnp.float32
@@ -101,12 +103,13 @@
     )(raw)
 
 
-def local_kernel(kernel, shapes, *args):
+def local_kernel(kernel, shapes, *args, scratch=()):
     return pl.pallas_call(
         kernel,
         in_specs=[VMEM] * len(args),
         out_specs=[VMEM] * len(shapes),
         out_shape=[jax.ShapeDtypeStruct(s, t) for s, t in shapes],
+        scratch_shapes=[pltpu.VMEM(s, t) for s, t in scratch],
         compiler_params=pltpu.CompilerParams(vmem_limit_bytes=VMEM_LIMIT),
         cost_estimate=pl.CostEstimate(
             flops=0, bytes_accessed=sum(a.size * a.dtype.itemsize for a in args), transcendentals=0
@@ -132,6 +135,30 @@
 
 def last_kernel(sum_ref, far_ref, out_ref):
     out_ref[...] = (sum_ref[...] + far_ref[...].astype(F32)).astype(BF16)
+
+
+def list_kernel(bands_ref, counts_ref, _, hot_ref, ranks_ref, pick_ref):
+    blocks = bands_ref.shape[1]
+    for k in range(blocks // LANES):
+        some = pl.ds(k * LANES, LANES)
+        slots = lax.broadcasted_iota(jnp.int32, (KMAX, LANES), 0)
+        place = jnp.where(slots < counts_ref[:, some], bands_ref[:, some], -LANES)
+        freqs = lax.broadcasted_iota(jnp.int32, (SEG, LANES), 0)
+        rank = jnp.zeros((SEG, LANES), jnp.int32)
+        for j in range(KMAX):
+            rank = jnp.where(freqs == place[j : j + 1], j + 1, rank)
+        rank = rank.astype(F32)
+        rank = jnp.concatenate([rank, rank], axis=0).T
+        place = place.astype(F32)
+        place = jnp.concatenate([place, place + SEG, place, place + SEG], axis=0).T
+        hot_ref[some, :] = rank
+        first = lax.broadcasted_iota(jnp.int32, (SUB, LANES), 1) < SEG
+        for p in range(LANES // (2 * SUB)):
+            at = p * 2 * SUB
+            out = pl.ds(k * (LANES // 2) + p * SUB, SUB)
+            ranks_ref[out, :] = jnp.where(first, rank[at : at + SUB], rank[at + SUB : at + 2 * SUB])
+            both = jnp.where(first, place[at : at + SUB], place[at + SUB : at + 2 * SUB])
+            pick_ref[out, :] = both.astype(jnp.int32)
 
 
 def base_kernel(mom_ref, mine_ref, given_ref, low_ref, high_ref, hot_ref, fwd_ref, inv_ref, out_ref, mask_ref):
@@ -146,8 +173,8 @@
         )
     blocks = hot_ref.shape[0]
     hot = hot_ref[...].astype(F32)
-    for q in range(GROUP // 2):
-        mask_ref[pl.ds(q, blocks, stride=GROUP // 2), :] = hot
+    for q in range(QUADS):
+        mask_ref[pl.ds(q, blocks, stride=QUADS), :] = hot
 
 
 def guess_kernel(base_ref, fwd_ref, coeff_ref):
@@ -158,14 +185,33 @@
         coeff_ref[some, :] = product(split(base_ref[some, :]), fwd_ref[...])
 
 
-def keep_kernel(coeff_ref, low_ref, high_ref, mask_ref, fwd_ref, sent_ref):
+def lane_gather(x, index):
+    return jnp.take_along_axis(x, index, axis=1, mode="promise_in_bounds")
+
+
+def keep_kernel(coeff_ref, low_ref, high_ref, mask_ref, pick_ref, rank_ref, fwd_ref, sent_ref, pack_ref, held_ref):
     half = low_ref.shape[0]
+    piece = 2 * SUB * QUADS
     step = min(half, 256)
+    first = lax.broadcasted_iota(jnp.int32, (SUB, LANES), 1) < SEG
     for at, part in ((0, low_ref), (half, high_ref)):
         for k in range(half // step):
-            some = pl.ds(at + k * step, step)
+            start = at + k * step
+            some = pl.ds(start, step)
             coeff = coeff_ref[some, :] + product(part[pl.ds(k * step, step), :], fwd_ref[:LANES, :])
+            held_ref[some, :] = coeff
             sent_ref[some, :] = jnp.where(mask_ref[some, :] > 0.5, coeff, 0.0).astype(BF16)
+            for p in range(start // piece, (start + step) // piece):
+                pick = pick_ref[pl.ds(p * SUB, SUB), :]
+                index = jnp.maximum(pick, 0)
+                out = []
+                for q in range(QUADS):
+                    one = held_ref[pl.ds(p * piece + q, SUB, stride=QUADS), :]
+                    two = held_ref[pl.ds(p * piece + piece // 2 + q, SUB, stride=QUADS), :]
+                    both = jnp.where(first, lane_gather(one, index), lane_gather(two, index))
+                    out.append(jnp.where(pick >= 0, both, 0.0))
+                out.append(rank_ref[pl.ds(p * SUB, SUB), :])
+                pack_ref[p] = jnp.concatenate(out, axis=0).astype(BF16)
 
 
 def remove_kernel(sent_ref, base_ref, low_ref, high_ref, inv_ref, new_ref):
@@ -178,10 +224,26 @@
             new_ref[some, :] = moment - product(sent_ref[some, :], inv_ref[:LANES, :])
 
 
-def combine_kernel(factor, pieces_ref, inv_ref, out_ref):
-    total = jnp.sum(pieces_ref[...].astype(F32), axis=0)
-    back = product(split(total), inv_ref[...]) * factor
-    out_ref[...] = jnp.broadcast_to(back.astype(BF16)[None], out_ref.shape)
+def combine_kernel(factor, pieces_ref, inv_ref, out_ref, held_ref):
+    first = lax.broadcasted_iota(jnp.int32, (SUB, LANES), 1) < SEG
+    shift = jnp.where(first, -1, KMAX - 1)
+    totals = [jnp.zeros((SUB, LANES), F32) for _ in range(2 * QUADS)]
+    for r in range(pieces_ref.shape[0]):
+        piece = pieces_ref[r].astype(F32)
+        rank = piece[SUB * QUADS :]
+        other = pltpu.roll(rank, SEG, axis=1)
+        for h in range(2):
+            place = jnp.where(first, rank, other) if h == 0 else jnp.where(first, other, rank)
+            index = jnp.maximum(place.astype(jnp.int32) + shift, 0) + h * SEG
+            for q in range(QUADS):
+                value = lane_gather(piece[q * SUB : (q + 1) * SUB], index)
+                totals[h * QUADS + q] += jnp.where(place > 0.5, value, 0.0)
+    back = product(split(jnp.concatenate(totals, axis=0)), inv_ref[...]) * factor
+    for h in range(2):
+        for q in range(QUADS):
+            at = (h * QUADS + q) * SUB
+            held_ref[pl.ds(h * SUB * QUADS + q, SUB, stride=QUADS), :] = back[at : at + SUB]
+    out_ref[...] = jnp.broadcast_to(held_ref[...].astype(BF16)[None], out_ref.shape)
 
 
 def spread_kernel(zs, *refs):
@@ -202,16 +264,6 @@
     rows = momentum.size // LANES
     half = rows // 2
 
-    freqs = jnp.arange(SEG, dtype=jnp.int32)
-    slots = jnp.arange(KMAX, dtype=jnp.int32)
-    lists = bands.reshape(blocks, KMAX)
-    live = counts.reshape(blocks)
-    hot = jnp.any(
-        (lists[:, :, None] == freqs[None, None, :]) & (slots[None, :, None] < live[:, None, None]),
-        axis=1,
-    ).astype(BF16)
-    hot = jnp.concatenate([hot, hot], axis=1)
-
     whole, part = (rows, LANES), (half, LANES)
 
     def over_cores(x):
@@ -237,6 +289,18 @@
     last_low = trade(last3, 3)
     (last1,) = local_kernel(last_kernel, [(part, BF16)], sum1, far3)
     last_high = trade(last1, 1)
+
+    hot, ranks, pick = pl.pallas_call(
+        list_kernel,
+        in_specs=[VMEM, VMEM, pl.BlockSpec(memory_space=pl.ANY)],
+        out_specs=[VMEM] * 3,
+        out_shape=[
+            jax.ShapeDtypeStruct((blocks, LANES), F32),
+            jax.ShapeDtypeStruct((blocks // 2, LANES), F32),
+            jax.ShapeDtypeStruct((blocks // 2, LANES), jnp.int32),
+        ],
+        compiler_params=pltpu.CompilerParams(vmem_limit_bytes=VMEM_LIMIT),
+    )(bands.reshape(blocks, KMAX).T, counts, near_low)
 
     base, mask = local_kernel(
         base_kernel,
@@ -251,19 +315,29 @@
         inverse,
     )
     (coeff,) = local_kernel(guess_kernel, [(whole, F32)], base, forward)
-    (sent,) = local_kernel(keep_kernel, [(whole, BF16)], coeff, last_low, last_high, mask, forward)
+    sent, pack = local_kernel(
+        keep_kernel,
+        [(whole, BF16), ((replicas, SUB * (QUADS + 1), LANES), BF16)],
+        coeff,
+        last_low,
+        last_high,
+        mask,
+        pick,
+        ranks,
+        forward,
+        scratch=[(whole, F32)],
+    )
     (new,) = local_kernel(remove_kernel, [(whole, F32)], sent, base, last_low, last_high, inverse)
 
-    pieces = lax.all_to_all(
-        sent.reshape(replicas, rows // replicas, LANES), "rep", split_axis=0, concat_axis=0, tiled=True
-    )
+    pieces = lax.all_to_all(pack, "rep", split_axis=0, concat_axis=0, tiled=True)
     xs = 4
     zs = replicas // xs
     (mixed,) = local_kernel(
         lambda *refs: combine_kernel(1.0 / math.sqrt(replicas), *refs),
-        [((zs,) + pieces.shape[1:], BF16)],
+        [((zs, 2 * SUB * QUADS, LANES), BF16)],
         pieces,
         inverse,
+        scratch=[((2 * SUB * QUADS, LANES), F32)],
     )
     lines = [[zs * x + z for z in range(zs)] for x in range(xs)]
     plane = lax.all_to_all(

time: 79.8 us -> 75.3 us (0.944)
  blocking collectives: 40.7 us -> 36.2 us
  waiting for transfers between devices: 13.5 us -> 15.7 us
  Pallas kernels: 8.46 us -> 6.87 us
  other arithmetic: 0.99 us -> 0 us
    all_to_all x1, blocking collectives: 27.9 us -> 23.7 us  [body(): lax.all_to_all(pack, 'rep', split_axis=0, concat_axis=0, tiled=True)]
    ppermute x6, waiting for transfers between devices: 10.5 us -> 12.7 us  [trade(): return lax.ppermute(x, 'fsdp', [(f, f ^ CORES * n) for f in range(holders)])]
    pallas_call x10, Pallas kernels: 6.36 us -> 5.05 us  [local_kernel(): pl.pallas_call(kernel, in_specs=[VMEM] * len(args), out_specs=[VMEM] * le...]
    reduce_or x1 -> x0, other arithmetic: 0.83 us -> none  [body(): jnp.any((lists[:, :, None] == freqs[None, None, :]) & (slots[None, :, Non...]
  transfers between devices with their start and end apart: 13 -> 13, of which waited for: 7 -> 7; matrix products, arithmetic and copies ran while one was open for 1% -> 0% of each run, Pallas kernels for 8% -> 6%
where the time goes in v3:
time: 75.3 us; the launch traced here: 75.2 us
  blocking collectives  36.2 us (48%)
  waiting for transfers between devices  15.7 us (21%)
  starting transfers between devices  12.2 us (16%)
  Pallas kernels  6.87 us (9%)
  local copies, waits for them, and re-layouts  3.41 us (5%)
  between operations  0.78 us (1%)
    all_to_all x1, blocking collectives, body(): lax.all_to_all(pack, 'rep', split_axis=0, concat_axis=0, tiled=True)  23.7 us
    ppermute x6, waiting for transfers between devices, trade(): return lax.ppermute(x, 'fsdp', [(f, f ^ CORES * n) for f in range(holders)])  12.7 us
    all_to_all x1, blocking collectives, body(): lax.all_to_all(mixed, 'rep', split_axis=0, concat_axis=0, axis_index_grou...  12.5 us
    ppermute x6, starting transfers between devices, trade(): return lax.ppermute(x, 'fsdp', [(f, f ^ CORES * n) for f in range(holders)])  6.97 us
    pallas_call x10, Pallas kernels, local_kernel(): pl.pallas_call(kernel, in_specs=[VMEM] * len(args), out_specs=[VMEM] * le...  5.05 us
    ppermute x3, starting transfers between devices, across(): lax.ppermute(plane, 'rep', [(r, r ^ zs * n) for r in range(replicas)])  4.09 us
    unnamed x12, local copies, waits for them, and re-layouts  3.41 us
    ppermute x3, waiting for transfers between devices, across(): lax.ppermute(plane, 'rep', [(r, r ^ zs * n) for r in range(replicas)])  2.95 us
  transfers between devices with their start and end apart: 13, of which 7 were waited for; matrix products, arithmetic and copies ran while one was open for 0% of the time, Pallas kernels for 6%

profile of v3, /device:TPU:24, one launch (start us, length us, event | category | flops | bytes accessed | tf_op | source)
XLA Modules:
  0.0 75.2 jit_solution(15669830207494363332)
XLA Ops:
  0.6 3.4 %copy-done = bf16[1,1,2097152]{2,1,0:T(2,128)(2,1)S(1)} copy-done((bf16[1,1,2097152]{2,1,0:T(2,128)(2,1)S(1)}, bf16[1,1,2097152]{2,1,0:T(2,128)(2,1)}, u32[]{:S(2)}) %copy-start) | copy-done | bytes 4194328
  4.0 0.2 shard_map.82
  4.3 1.2 %shard_map.77 = (bf16[2048,128]{1,0:T(8,128)(2,1)S(1)}, bf16[2048,128]{1,0:T(8,128)(2,1)S(1)}, bf16[2048,128]{1,0:T(8,128)(2,1)S(1)}, bf16[2048,128]{1,0:T(8,128...) custom-call(bf16[1,1,2097152]{2,1,0:T(2,128)(2,1)S(1)} %copy-done), custom_call_target="tpu_custom_call" | custom-call | bytes 11010048 | tf_op jit(solution)/shard_map/pallas_call | solution.py:92
  5.5 0.6 collective-permute-start.1
  6.1 0.1 collective-permute-start.2
  6.2 0.4 collective-permute-start
  6.6 0.1 shard_map.83
  6.7 0.8 %collective-permute-start.6 = (bf16[1024,128]{1,0:T(8,128)(2,1)S(1)}, bf16[1024,128]{1,0:T(8,128)(2,1)S(1)}, u32[]{:S(2)}, u32[]{:S(2)}) collective-permute-start(bf16[1024,128]{1,0:T(8,128)(2,1)S(1)} %get-tuple-element.34), channel_id=1, source_target_pairs={{0,2},{1,3},{2,0},{3,1},{4,6},{5,7},{6,4},{7,5},{8,10},{9,11},{10,... | collective-permute-start | bytes 786440 | tf_op jit(solution)/shard_map/ppermute | solution.py:273
  7.6 1.3 %collective-permute-start.8 = (bf16[1024,128]{1,0:T(8,128)(2,1)S(1)}, bf16[1024,128]{1,0:T(8,128)(2,1)S(1)}, u32[]{:S(2)}, u32[]{:S(2)}) collective-permute-start(bf16[1024,128]{1,0:T(8,128)(2,1)S(1)} %get-tuple-element.36), channel_id=1, source_target_pairs={{0,6},{1,7},{2,4},{3,5},{4,2},{5,3},{6,0},{7,1},{8,14},{9,15},{10,... | collective-permute-start | bytes 786440 | tf_op jit(solution)/shard_map/ppermute | solution.py:273
  8.9 0.2 shard_map.78
  9.1 1.4 %collective-permute-start.3 = (bf16[1024,128]{1,0:T(8,128)(2,1)S(1)}, bf16[1024,128]{1,0:T(8,128)(2,1)S(1)}, u32[]{:S(2)}, u32[]{:S(2)}) collective-permute-start(bf16[1024,128]{1,0:T(8,128)(2,1)S(1)} %get-tuple-element.28), channel_id=1, source_target_pairs={{0,2},{1,3},{2,0},{3,1},{4,6},{5,7},{6,4},{7,5},{8,10},{9,11},{10,... | collective-permute-start | bytes 786440 | tf_op jit(solution)/shard_map/ppermute | solution.py:273
  10.5 1.3 %collective-permute-start.4 = (bf16[1024,128]{1,0:T(8,128)(2,1)S(1)}, bf16[1024,128]{1,0:T(8,128)(2,1)S(1)}, u32[]{:S(2)}, u32[]{:S(2)}) collective-permute-start(bf16[1024,128]{1,0:T(8,128)(2,1)S(1)} %get-tuple-element.29), channel_id=1, source_target_pairs={{0,6},{1,7},{2,4},{3,5},{4,2},{5,3},{6,0},{7,1},{8,14},{9,15},{10,... | collective-permute-start | bytes 786440 | tf_op jit(solution)/shard_map/ppermute | solution.py:273
  11.8 4.2 %collective-permute-done.6.far_ref = bf16[1024,128]{1,0:T(8,128)(2,1)S(1)} collective-permute-done((bf16[1024,128]{1,0:T(8,128)(2,1)S(1)}, bf16[1024,128]{1,0:T(8,128)(2,1)S(1)}, u32[]{:S(2)}, u32[]{:S(2)}) %collective-permute-start.6) | collective-permute-done | bytes 262176 | tf_op jit(solution)/shard_map/ppermute | solution.py:273
  16.0 2.0 %collective-permute-start.7 = (bf16[1024,128]{1,0:T(8,128)(2,1)S(1)}, bf16[1024,128]{1,0:T(8,128)(2,1)S(1)}, u32[]{:S(2)}, u32[]{:S(2)}) collective-permute-start(bf16[1024,128]{1,0:T(8,128)(2,1)S(1)} %shard_map.84), channel_id=1, source_target_pairs={{0,6},{1,7},{2,4},{3,5},{4,2},{5,3},{6,0},{7,1},{8,14},{9,15},{10,... | collective-permute-start | bytes 786440 | tf_op jit(solution)/shard_map/ppermute | solution.py:273
  18.2 3.4 %collective-permute-done.3._.low_ref = bf16[1024,128]{1,0:T(8,128)(2,1)S(1)} collective-permute-done((bf16[1024,128]{1,0:T(8,128)(2,1)S(1)}, bf16[1024,128]{1,0:T(8,128)(2,1)S(1)}, u32[]{:S(2)}, u32[]{:S(2)}) %collective-permute-start.3) | collective-permute-done | bytes 262176 | tf_op jit(solution)/shard_map/ppermute | solution.py:273
  21.6 0.5 shard_map.79
  22.1 1.5 %collective-permute-done.4.high_ref = bf16[1024,128]{1,0:T(8,128)(2,1)S(1)} collective-permute-done((bf16[1024,128]{1,0:T(8,128)(2,1)S(1)}, bf16[1024,128]{1,0:T(8,128)(2,1)S(1)}, u32[]{:S(2)}, u32[]{:S(2)}) %collective-permute-start.4) | collective-permute-done | bytes 262176 | tf_op jit(solution)/shard_map/ppermute | solution.py:273
  23.6 0.3 shard_map.80
  23.9 0.5 shard_map.81.coeff_ref
  24.4 3.7 %collective-permute-done.7.low_ref = bf16[1024,128]{1,0:T(8,128)(2,1)S(1)} collective-permute-done((bf16[1024,128]{1,0:T(8,128)(2,1)S(1)}, bf16[1024,128]{1,0:T(8,128)(2,1)S(1)}, u32[]{:S(2)}, u32[]{:S(2)}) %collective-permute-start.7) | collective-permute-done | bytes 262176 | tf_op jit(solution)/shard_map/ppermute | solution.py:273
  28.0 0.5 shard_map.86
  28.6 23.7 %all_to_all.10.refs_0_ = bf16[32,40,128]{2,1,0:T(8,128)(2,1)S(1)} all-to-all(bf16[32,40,128]{2,1,0:T(8,128)(2,1)S(1)} %get-tuple-element.41), channel_id=1, replica_groups=mesh['rep'=32,'fsdp'=8] {'rep'}, dimensions={0} | all-to-all | bytes 655360 | tf_op jit(solution)/shard_map/all_to_all | solution.py:332
  52.2 0.9 %shard_map.88 = bf16[8,64,128]{2,1,0:T(8,128)(2,1)S(1)} custom-call(bf16[32,40,128]{2,1,0:T(8,128)(2,1)S(1)} %all_to_all.10.refs_0_, bf16[256,256]{1,0:T(8,128)(2,1)S(1)} %copy-done.2), custom_call_target="tpu_custom_call" | custom-call | bytes 458752 | tf_op jit(solution)/shard_map/pallas_call | solution.py:107
  53.1 12.5 %all_to_all.11 = bf16[8,64,128]{2,1,0:T(8,128)(2,1)S(1)} all-to-all(bf16[8,64,128]{2,1,0:T(8,128)(2,1)S(1)} %shard_map.88), channel_id=1, replica_groups={{0,8,16,24,32,40,48,56},{64,72,80,88,96,104,112,120},{128,136,144,152,1..., dimensions={0} | all-to-all | bytes 262144 | tf_op jit(solution)/shard_map/all_to_all | solution.py:343
  65.7 1.2 %collective-permute-start.12 = (bf16[512,128]{1,0:T(8,128)(2,1)S(1)}, bf16[512,128]{1,0:T(8,128)(2,1)S(1)}, u32[]{:S(2)}, u32[]{:S(2)}) collective-permute-start(bf16[512,128]{1,0:T(8,128)(2,1)S(1)} %bitcast.8), channel_id=1, source_target_pairs={{0,192},{8,200},{16,208},{24,216},{32,224},{40,232},{48,240},{56,2... | collective-permute-start | bytes 393224 | tf_op jit(solution)/shard_map/ppermute | solution.py:348
  66.8 1.5 %collective-permute-start.11 = (bf16[512,128]{1,0:T(8,128)(2,1)S(1)}, bf16[512,128]{1,0:T(8,128)(2,1)S(1)}, u32[]{:S(2)}, u32[]{:S(2)}) collective-permute-start(bf16[512,128]{1,0:T(8,128)(2,1)S(1)} %bitcast.9), channel_id=1, source_target_pairs={{0,128},{8,136},{16,144},{24,152},{32,160},{40,168},{48,176},{56,1... | collective-permute-start | bytes 393224 | tf_op jit(solution)/shard_map/ppermute | solution.py:348
  68.3 1.4 %collective-permute-start.10 = (bf16[512,128]{1,0:T(8,128)(2,1)S(1)}, bf16[512,128]{1,0:T(8,128)(2,1)S(1)}, u32[]{:S(2)}, u32[]{:S(2)}) collective-permute-start(bf16[512,128]{1,0:T(8,128)(2,1)S(1)} %bitcast.10), channel_id=1, source_target_pairs={{0,64},{8,72},{16,80},{24,88},{32,96},{40,104},{48,112},{56,120},{... | collective-permute-start | bytes 393224 | tf_op jit(solution)/shard_map/ppermute | solution.py:348
  69.8 1.4 %shard_map.87 = f32[2048,128]{1,0:T(8,128)} custom-call(bf16[2048,128]{1,0:T(8,128)(2,1)S(1)} %get-tuple-element.40.sent_ref, f32[2048,128]{1,0:T(8,128)S(1)} %get-tuple-element.31.base_ref, bf16[1024,128]{1,0:T(8,128)(2,1)S(1)} %collective-permute-done.7.low_ref, bf16[1024,128]{1,0:T(8,128)(2,1)S(1)} %collective-permute-done.9.high_ref, ...), custom_call_target="tpu_custom_call" | custom-call | bytes 2228224 | tf_op jit(solution)/shard_map/pallas_call | solution.py:107
  71.1 0.7 collective-permute-done.12.refs_3_
  71.8 1.5 %collective-permute-done.11.refs_2_ = bf16[512,128]{1,0:T(8,128)(2,1)S(1)} collective-permute-done((bf16[512,128]{1,0:T(8,128)(2,1)S(1)}, bf16[512,128]{1,0:T(8,128)(2,1)S(1)}, u32[]{:S(2)}, u32[]{:S(2)}) %collective-permute-start.11) | collective-permute-done | bytes 131104 | tf_op jit(solution)/shard_map/ppermute | solution.py:348
  73.3 0.8 %collective-permute-done.10.refs_1_ = bf16[512,128]{1,0:T(8,128)(2,1)S(1)} collective-permute-done((bf16[512,128]{1,0:T(8,128)(2,1)S(1)}, bf16[512,128]{1,0:T(8,128)(2,1)S(1)}, u32[]{:S(2)}, u32[]{:S(2)}) %collective-permute-start.10) | collective-permute-done | bytes 131104 | tf_op jit(solution)/shard_map/ppermute | solution.py:348
  74.1 1.1 %shard_map.89 = f32[2048,128]{1,0:T(8,128)} custom-call(bf16[512,128]{1,0:T(8,128)(2,1)S(1)} %bitcast.11, bf16[512,128]{1,0:T(8,128)(2,1)S(1)} %collective-permute-done.10.refs_1_, bf16[512,128]{1,0:T(8,128)(2,1)S(1)} %collective-permute-done.11.refs_2_, bf16[512,128]{1,0:T(8,128)(2,1)S(1)} %collective-permute-done.12.refs_3_), custom_call_target="tpu_custom_call" | custom-call | bytes 524288 | tf_op jit(solution)/shard_map/pallas_call | solution.py:107
  (21 shorter events, 0.3 us)
Async XLA Ops:
  0.6 3.4 %copy-start = (bf16[1,1,2097152]{2,1,0:T(2,128)(2,1)S(1)}, bf16[1,1,2097152]{2,1,0:T(2,128)(2,1)}, u32[]{:S(2)}) copy-start(bf16[1,1,2097152]{2,1,0:T(2,128)(2,1)} %raw_ref.3) | copy-start | bytes 12582916
  4.2 17.4 %copy-start.4 = (s32[1,512,32]{1,2,0:T(8,128)S(1)}, s32[1,512,32]{1,2,0:T(8,128)}, u32[]{:S(2)}) copy-start(s32[1,512,32]{1,2,0:T(8,128)} %param.8) | copy-start | bytes 196612
  4.2 17.4 %copy-start.5 = (s32[1,512]{1,0:T(1,128)S(1)}, s32[1,512]{1,0:T(1,128)}, u32[]{:S(2)}) copy-start(s32[1,512]{1,0:T(1,128)} %counts_ref.1) | copy-start | bytes 6148
  4.2 19.4 %copy-start.1 = (bf16[256,256]{1,0:T(8,128)(2,1)S(1)}, bf16[256,256]{1,0:T(8,128)(2,1)}, u32[]{:S(2)}) copy-start(bf16[256,256]{1,0:T(8,128)(2,1)} %constant.4.clone.fwd_ref) | copy-start | bytes 393220
  4.2 19.4 %copy-start.2 = (bf16[256,256]{1,0:T(8,128)(2,1)S(1)}, bf16[256,256]{1,0:T(8,128)(2,1)}, u32[]{:S(2)}) copy-start(bf16[256,256]{1,0:T(8,128)(2,1)} %constant.5.clone.inv_ref.refs_1_) | copy-start | bytes 393220
  4.2 19.4 %copy-start.3 = (f32[1,262144]{1,0:T(1,128)S(1)}, f32[1,262144]{1,0:T(1,128)}, u32[]{:S(2)}) copy-start(f32[1,262144]{1,0:T(1,128)} %param.7) | copy-start | bytes 3145732
  4.2 2.4 %collective-permute-start.5 = (bf16[2048,128]{1,0:T(8,128)(2,1)S(1)}, bf16[2048,128]{1,0:T(8,128)(2,1)S(1)}, u32[]{:S(2)}, u32[]{:S(2)}) collective-permute-start(bf16[2048,128]{1,0:T(8,128)(2,1)S(1)} %shard_map.82), channel_id=1, source_target_pairs={{0,1},{1,0},{2,3},{3,2},{4,5},{5,4},{6,7},{7,6},{8,9},{9,8},{10,11... | collective-permute-start | bytes 1572872 | tf_op jit(solution)/shard_map/ppermute | solution.py:270
  5.5 3.3 %collective-permute-start.1 = (bf16[2048,128]{1,0:T(8,128)(2,1)S(1)}, bf16[2048,128]{1,0:T(8,128)(2,1)S(1)}, u32[]{:S(2)}, u32[]{:S(2)}) collective-permute-start(bf16[2048,128]{1,0:T(8,128)(2,1)S(1)} %get-tuple-element.25), channel_id=1, source_target_pairs={{0,1},{1,0},{2,3},{3,2},{4,5},{5,4},{6,7},{7,6},{8,9},{9,8},{10,11... | collective-permute-start | bytes 1572872 | tf_op jit(solution)/shard_map/ppermute | solution.py:270
  6.1 2.8 %collective-permute-start.2 = (bf16[2048,128]{1,0:T(8,128)(2,1)S(1)}, bf16[2048,128]{1,0:T(8,128)(2,1)S(1)}, u32[]{:S(2)}, u32[]{:S(2)}) collective-permute-start(bf16[2048,128]{1,0:T(8,128)(2,1)S(1)} %get-tuple-element.27), channel_id=1, source_target_pairs={{0,1},{1,0},{2,3},{3,2},{4,5},{5,4},{6,7},{7,6},{8,9},{9,8},{10,11... | collective-permute-start | bytes 1572872 | tf_op jit(solution)/shard_map/ppermute | solution.py:270
  6.2 15.9 %collective-permute-start = (bf16[2048,128]{1,0:T(8,128)(2,1)S(1)}, bf16[2048,128]{1,0:T(8,128)(2,1)S(1)}, u32[]{:S(2)}, u32[]{:S(2)}) collective-permute-start(bf16[2048,128]{1,0:T(8,128)(2,1)S(1)} %get-tuple-element.23), channel_id=1, source_target_pairs={{0,1},{1,0},{2,3},{3,2},{4,5},{5,4},{6,7},{7,6},{8,9},{9,8},{10,11... | collective-permute-start | bytes 1572872 | tf_op jit(solution)/shard_map/ppermute | solution.py:270
  6.7 9.2 %collective-permute-start.6 = (bf16[1024,128]{1,0:T(8,128)(2,1)S(1)}, bf16[1024,128]{1,0:T(8,128)(2,1)S(1)}, u32[]{:S(2)}, u32[]{:S(2)}) collective-permute-start(bf16[1024,128]{1,0:T(8,128)(2,1)S(1)} %get-tuple-element.34), channel_id=1, source_target_pairs={{0,2},{1,3},{2,0},{3,1},{4,6},{5,7},{6,4},{7,5},{8,10},{9,11},{10,... | collective-permute-start | bytes 786440 | tf_op jit(solution)/shard_map/ppermute | solution.py:273
  7.6 10.5 %collective-permute-start.8 = (bf16[1024,128]{1,0:T(8,128)(2,1)S(1)}, bf16[1024,128]{1,0:T(8,128)(2,1)S(1)}, u32[]{:S(2)}, u32[]{:S(2)}) collective-permute-start(bf16[1024,128]{1,0:T(8,128)(2,1)S(1)} %get-tuple-element.36), channel_id=1, source_target_pairs={{0,6},{1,7},{2,4},{3,5},{4,2},{5,3},{6,0},{7,1},{8,14},{9,15},{10,... | collective-permute-start | bytes 786440 | tf_op jit(solution)/shard_map/ppermute | solution.py:273
  9.1 12.5 %collective-permute-start.3 = (bf16[1024,128]{1,0:T(8,128)(2,1)S(1)}, bf16[1024,128]{1,0:T(8,128)(2,1)S(1)}, u32[]{:S(2)}, u32[]{:S(2)}) collective-permute-start(bf16[1024,128]{1,0:T(8,128)(2,1)S(1)} %get-tuple-element.28), channel_id=1, source_target_pairs={{0,2},{1,3},{2,0},{3,1},{4,6},{5,7},{6,4},{7,5},{8,10},{9,11},{10,... | collective-permute-start | bytes 786440 | tf_op jit(solution)/shard_map/ppermute | solution.py:273
  10.5 13.1 %collective-permute-start.4 = (bf16[1024,128]{1,0:T(8,128)(2,1)S(1)}, bf16[1024,128]{1,0:T(8,128)(2,1)S(1)}, u32[]{:S(2)}, u32[]{:S(2)}) collective-permute-start(bf16[1024,128]{1,0:T(8,128)(2,1)S(1)} %get-tuple-element.29), channel_id=1, source_target_pairs={{0,6},{1,7},{2,4},{3,5},{4,2},{5,3},{6,0},{7,1},{8,14},{9,15},{10,... | collective-permute-start | bytes 786440 | tf_op jit(solution)/shard_map/ppermute | solution.py:273
  16.0 12.0 %collective-permute-start.7 = (bf16[1024,128]{1,0:T(8,128)(2,1)S(1)}, bf16[1024,128]{1,0:T(8,128)(2,1)S(1)}, u32[]{:S(2)}, u32[]{:S(2)}) collective-permute-start(bf16[1024,128]{1,0:T(8,128)(2,1)S(1)} %shard_map.84), channel_id=1, source_target_pairs={{0,6},{1,7},{2,4},{3,5},{4,2},{5,3},{6,0},{7,1},{8,14},{9,15},{10,... | collective-permute-start | bytes 786440 | tf_op jit(solution)/shard_map/ppermute | solution.py:273
  18.1 9.9 %collective-permute-start.9 = (bf16[1024,128]{1,0:T(8,128)(2,1)S(1)}, bf16[1024,128]{1,0:T(8,128)(2,1)S(1)}, u32[]{:S(2)}, u32[]{:S(2)}) collective-permute-start(bf16[1024,128]{1,0:T(8,128)(2,1)S(1)} %shard_map.85), channel_id=1, source_target_pairs={{0,2},{1,3},{2,0},{3,1},{4,6},{5,7},{6,4},{7,5},{8,10},{9,11},{10,... | collective-permute-start | bytes 786440 | tf_op jit(solution)/shard_map/ppermute | solution.py:273
  65.7 6.2 %collective-permute-start.12 = (bf16[512,128]{1,0:T(8,128)(2,1)S(1)}, bf16[512,128]{1,0:T(8,128)(2,1)S(1)}, u32[]{:S(2)}, u32[]{:S(2)}) collective-permute-start(bf16[512,128]{1,0:T(8,128)(2,1)S(1)} %bitcast.8), channel_id=1, source_target_pairs={{0,192},{8,200},{16,208},{24,216},{32,224},{40,232},{48,240},{56,2... | collective-permute-start | bytes 393224 | tf_op jit(solution)/shard_map/ppermute | solution.py:348
  66.8 6.5 %collective-permute-start.11 = (bf16[512,128]{1,0:T(8,128)(2,1)S(1)}, bf16[512,128]{1,0:T(8,128)(2,1)S(1)}, u32[]{:S(2)}, u32[]{:S(2)}) collective-permute-start(bf16[512,128]{1,0:T(8,128)(2,1)S(1)} %bitcast.9), channel_id=1, source_target_pairs={{0,128},{8,136},{16,144},{24,152},{32,160},{40,168},{48,176},{56,1... | collective-permute-start | bytes 393224 | tf_op jit(solution)/shard_map/ppermute | solution.py:348
  68.3 5.8 %collective-permute-start.10 = (bf16[512,128]{1,0:T(8,128)(2,1)S(1)}, bf16[512,128]{1,0:T(8,128)(2,1)S(1)}, u32[]{:S(2)}, u32[]{:S(2)}) collective-permute-start(bf16[512,128]{1,0:T(8,128)(2,1)S(1)} %bitcast.10), channel_id=1, source_target_pairs={{0,64},{8,72},{16,80},{24,88},{32,96},{40,104},{48,112},{56,120},{... | collective-permute-start | bytes 393224 | tf_op jit(solution)/shard_map/ppermute | solution.py:348

commit v4 on v3

--- a/solution.py
+++ b/solution.py
@@ -59,45 +59,25 @@
     count = len(wanted)
     size = raw.shape[-1] // PIECES
     rows = size // LANES
-    cuts = 2
-    cut = size // cuts
-    lines = cut // LANES
-    step = min(lines, 128)
-
-    def kernel(raw_ref, *refs):
-        outs, (held, sems) = refs[:count], refs[count:]
+    step = min(rows, 128)
+
+    def kernel(raw_ref, *outs):
         me = lax.axis_index("fsdp")
         chip, core = me // CORES, lax.rem(me, CORES)
-
-        def fetch(i, j):
-            n, other = wanted[i]
+        for i, (n, other) in enumerate(wanted):
             lane = lax.rem(core + other, CORES)
             to = (chip, chip + 1 - 2 * lax.rem(chip, 2), lax.rem(chip + 2, 4), 3 - chip)[n]
-            piece = to * CORES + lane
-            at = pl.multiple_of(piece * size + j * cut, cut)
-            return pltpu.make_async_copy(
-                raw_ref.at[:, :, pl.ds(at, cut)], held.at[i * cuts + j], sems.at[i * cuts + j]
-            )
-
-        for i in range(count):
-            for j in range(cuts):
-                fetch(i, j).start()
-        for i in range(count):
-            for j in range(cuts):
-                fetch(i, j).wait()
-                for k in range(lines // step):
-                    some = held[i * cuts + j, 0, :, pl.ds(k * step * LANES, step * LANES)]
-                    outs[i][pl.ds(j * lines + k * step, step), :] = some.reshape(step, LANES)
+            start = (to * CORES + lane) * size
+            for k in range(rows // step):
+                at = pl.multiple_of(start + k * step * LANES, step * LANES)
+                some = raw_ref[0, :, pl.ds(at, step * LANES)]
+                outs[i][pl.ds(k * step, step), :] = some.reshape(step, LANES)
 
     return pl.pallas_call(
         kernel,
-        in_specs=[pl.BlockSpec(memory_space=pltpu.HBM)],
+        in_specs=[VMEM],
         out_specs=[VMEM] * count,
         out_shape=[jax.ShapeDtypeStruct((rows, LANES), BF16)] * count,
-        scratch_shapes=[
-            pltpu.VMEM((count * cuts, 1, 1, cut), BF16),
-            pltpu.SemaphoreType.DMA((count * cuts,)),
-        ],
         compiler_params=pltpu.CompilerParams(vmem_limit_bytes=VMEM_LIMIT),
         cost_estimate=pl.CostEstimate(flops=0, bytes_accessed=count * size * 6, transcendentals=0),
     )(raw)

time: 75.3 us -> 75 us (level)
  Pallas kernels: 6.87 us -> 6.11 us
    pallas_call x2, Pallas kernels: 1.34 us -> 0.59 us  [unpack(): pl.pallas_call(kernel, in_specs=[VMEM], out_specs=[VMEM] * count, out_sha...]
  transfers between devices with their start and end apart: 13 -> 13, of which waited for: 7 -> 8; matrix products, arithmetic and copies ran while one was open for 0% -> 0% of each run, Pallas kernels for 6% -> 5%
where the time goes in v4:
time: 75 us; the launch traced here: 74.8 us
  blocking collectives  36.2 us (48%)
  waiting for transfers between devices  16 us (21%)
  starting transfers between devices  12.2 us (16%)
  Pallas kernels  6.11 us (8%)
  local copies, waits for them, and re-layouts  3.41 us (5%)
  between operations  0.78 us (1%)
    all_to_all x1, blocking collectives, body(): lax.all_to_all(pack, 'rep', split_axis=0, concat_axis=0, tiled=True)  23.7 us
    ppermute x6, waiting for transfers between devices, trade(): return lax.ppermute(x, 'fsdp', [(f, f ^ CORES * n) for f in range(holders)])  12.8 us
    all_to_all x1, blocking collectives, body(): lax.all_to_all(mixed, 'rep', split_axis=0, concat_axis=0, axis_index_grou...  12.5 us
    ppermute x6, starting transfers between devices, trade(): return lax.ppermute(x, 'fsdp', [(f, f ^ CORES * n) for f in range(holders)])  6.97 us
    pallas_call x10, Pallas kernels, local_kernel(): pl.pallas_call(kernel, in_specs=[VMEM] * len(args), out_specs=[VMEM] * le...  5.04 us
    ppermute x3, starting transfers between devices, across(): lax.ppermute(plane, 'rep', [(r, r ^ zs * n) for r in range(replicas)])  4.09 us
    unnamed x12, local copies, waits for them, and re-layouts  3.41 us
    ppermute x3, waiting for transfers between devices, across(): lax.ppermute(plane, 'rep', [(r, r ^ zs * n) for r in range(replicas)])  2.95 us
  transfers between devices with their start and end apart: 13, of which 8 were waited for; matrix products, arithmetic and copies ran while one was open for 0% of the time, Pallas kernels for 5%

profile of v4, /device:TPU:24, one launch (start us, length us, event | category | flops | bytes accessed | tf_op | source)
XLA Modules:
  0.0 74.8 jit_solution(12316340550817541005)
XLA Ops:
  0.6 3.4 %copy-done = bf16[1,1,2097152]{2,1,0:T(2,128)(2,1)S(1)} copy-done((bf16[1,1,2097152]{2,1,0:T(2,128)(2,1)S(1)}, bf16[1,1,2097152]{2,1,0:T(2,128)(2,1)}, u32[]{:S(2)}) %copy-start) | copy-done | bytes 4194328
  4.2 0.5 shard_map.77
  4.8 0.6 collective-permute-start.1
  5.3 0.1 collective-permute-start.2
  5.4 0.4 collective-permute-start
  5.8 0.3 collective-permute-done.5.given_ref
  6.1 0.1 shard_map.83
  6.3 0.8 %collective-permute-start.6 = (bf16[1024,128]{1,0:T(8,128)(2,1)S(1)}, bf16[1024,128]{1,0:T(8,128)(2,1)S(1)}, u32[]{:S(2)}, u32[]{:S(2)}) collective-permute-start(bf16[1024,128]{1,0:T(8,128)(2,1)S(1)} %get-tuple-element.34), channel_id=1, source_target_pairs={{0,2},{1,3},{2,0},{3,1},{4,6},{5,7},{6,4},{7,5},{8,10},{9,11},{10,... | collective-permute-start | bytes 786440 | tf_op jit(solution)/shard_map/ppermute | solution.py:253
  7.1 1.3 %collective-permute-start.8 = (bf16[1024,128]{1,0:T(8,128)(2,1)S(1)}, bf16[1024,128]{1,0:T(8,128)(2,1)S(1)}, u32[]{:S(2)}, u32[]{:S(2)}) collective-permute-start(bf16[1024,128]{1,0:T(8,128)(2,1)S(1)} %get-tuple-element.36), channel_id=1, source_target_pairs={{0,6},{1,7},{2,4},{3,5},{4,2},{5,3},{6,0},{7,1},{8,14},{9,15},{10,... | collective-permute-start | bytes 786440 | tf_op jit(solution)/shard_map/ppermute | solution.py:253
  8.4 0.2 shard_map.78
  8.6 1.4 %collective-permute-start.3 = (bf16[1024,128]{1,0:T(8,128)(2,1)S(1)}, bf16[1024,128]{1,0:T(8,128)(2,1)S(1)}, u32[]{:S(2)}, u32[]{:S(2)}) collective-permute-start(bf16[1024,128]{1,0:T(8,128)(2,1)S(1)} %get-tuple-element.28), channel_id=1, source_target_pairs={{0,2},{1,3},{2,0},{3,1},{4,6},{5,7},{6,4},{7,5},{8,10},{9,11},{10,... | collective-permute-start | bytes 786440 | tf_op jit(solution)/shard_map/ppermute | solution.py:253
  10.1 1.3 %collective-permute-start.4 = (bf16[1024,128]{1,0:T(8,128)(2,1)S(1)}, bf16[1024,128]{1,0:T(8,128)(2,1)S(1)}, u32[]{:S(2)}, u32[]{:S(2)}) collective-permute-start(bf16[1024,128]{1,0:T(8,128)(2,1)S(1)} %get-tuple-element.29), channel_id=1, source_target_pairs={{0,6},{1,7},{2,4},{3,5},{4,2},{5,3},{6,0},{7,1},{8,14},{9,15},{10,... | collective-permute-start | bytes 786440 | tf_op jit(solution)/shard_map/ppermute | solution.py:253
  11.3 4.2 %collective-permute-done.6.far_ref = bf16[1024,128]{1,0:T(8,128)(2,1)S(1)} collective-permute-done((bf16[1024,128]{1,0:T(8,128)(2,1)S(1)}, bf16[1024,128]{1,0:T(8,128)(2,1)S(1)}, u32[]{:S(2)}, u32[]{:S(2)}) %collective-permute-start.6) | collective-permute-done | bytes 262176 | tf_op jit(solution)/shard_map/ppermute | solution.py:253
  15.6 2.0 %collective-permute-start.7 = (bf16[1024,128]{1,0:T(8,128)(2,1)S(1)}, bf16[1024,128]{1,0:T(8,128)(2,1)S(1)}, u32[]{:S(2)}, u32[]{:S(2)}) collective-permute-start(bf16[1024,128]{1,0:T(8,128)(2,1)S(1)} %shard_map.84), channel_id=1, source_target_pairs={{0,6},{1,7},{2,4},{3,5},{4,2},{5,3},{6,0},{7,1},{8,14},{9,15},{10,... | collective-permute-start | bytes 786440 | tf_op jit(solution)/shard_map/ppermute | solution.py:253
  17.8 3.4 %collective-permute-done.3._.low_ref = bf16[1024,128]{1,0:T(8,128)(2,1)S(1)} collective-permute-done((bf16[1024,128]{1,0:T(8,128)(2,1)S(1)}, bf16[1024,128]{1,0:T(8,128)(2,1)S(1)}, u32[]{:S(2)}, u32[]{:S(2)}) %collective-permute-start.3) | collective-permute-done | bytes 262176 | tf_op jit(solution)/shard_map/ppermute | solution.py:253
  21.1 0.5 shard_map.79
  21.6 1.5 %collective-permute-done.4.high_ref = bf16[1024,128]{1,0:T(8,128)(2,1)S(1)} collective-permute-done((bf16[1024,128]{1,0:T(8,128)(2,1)S(1)}, bf16[1024,128]{1,0:T(8,128)(2,1)S(1)}, u32[]{:S(2)}, u32[]{:S(2)}) %collective-permute-start.4) | collective-permute-done | bytes 262176 | tf_op jit(solution)/shard_map/ppermute | solution.py:253
  23.1 0.3 shard_map.80
  23.4 0.4 shard_map.81.coeff_ref
  23.9 3.7 %collective-permute-done.7.low_ref = bf16[1024,128]{1,0:T(8,128)(2,1)S(1)} collective-permute-done((bf16[1024,128]{1,0:T(8,128)(2,1)S(1)}, bf16[1024,128]{1,0:T(8,128)(2,1)S(1)}, u32[]{:S(2)}, u32[]{:S(2)}) %collective-permute-start.7) | collective-permute-done | bytes 262176 | tf_op jit(solution)/shard_map/ppermute | solution.py:253
  27.6 0.5 shard_map.86
  28.1 23.7 %all_to_all.10.refs_0_ = bf16[32,40,128]{2,1,0:T(8,128)(2,1)S(1)} all-to-all(bf16[32,40,128]{2,1,0:T(8,128)(2,1)S(1)} %get-tuple-element.41), channel_id=1, replica_groups=mesh['rep'=32,'fsdp'=8] {'rep'}, dimensions={0} | all-to-all | bytes 655360 | tf_op jit(solution)/shard_map/all_to_all | solution.py:312
  51.9 0.9 %shard_map.88 = bf16[8,64,128]{2,1,0:T(8,128)(2,1)S(1)} custom-call(bf16[32,40,128]{2,1,0:T(8,128)(2,1)S(1)} %all_to_all.10.refs_0_, bf16[256,256]{1,0:T(8,128)(2,1)S(1)} %copy-done.2), custom_call_target="tpu_custom_call" | custom-call | bytes 458752 | tf_op jit(solution)/shard_map/pallas_call | solution.py:87
  52.8 12.5 %all_to_all.11 = bf16[8,64,128]{2,1,0:T(8,128)(2,1)S(1)} all-to-all(bf16[8,64,128]{2,1,0:T(8,128)(2,1)S(1)} %shard_map.88), channel_id=1, replica_groups={{0,8,16,24,32,40,48,56},{64,72,80,88,96,104,112,120},{128,136,144,152,1..., dimensions={0} | all-to-all | bytes 262144 | tf_op jit(solution)/shard_map/all_to_all | solution.py:323
  65.3 1.2 %collective-permute-start.12 = (bf16[512,128]{1,0:T(8,128)(2,1)S(1)}, bf16[512,128]{1,0:T(8,128)(2,1)S(1)}, u32[]{:S(2)}, u32[]{:S(2)}) collective-permute-start(bf16[512,128]{1,0:T(8,128)(2,1)S(1)} %bitcast.8), channel_id=1, source_target_pairs={{0,192},{8,200},{16,208},{24,216},{32,224},{40,232},{48,240},{56,2... | collective-permute-start | bytes 393224 | tf_op jit(solution)/shard_map/ppermute | solution.py:328
  66.4 1.5 %collective-permute-start.11 = (bf16[512,128]{1,0:T(8,128)(2,1)S(1)}, bf16[512,128]{1,0:T(8,128)(2,1)S(1)}, u32[]{:S(2)}, u32[]{:S(2)}) collective-permute-start(bf16[512,128]{1,0:T(8,128)(2,1)S(1)} %bitcast.9), channel_id=1, source_target_pairs={{0,128},{8,136},{16,144},{24,152},{32,160},{40,168},{48,176},{56,1... | collective-permute-start | bytes 393224 | tf_op jit(solution)/shard_map/ppermute | solution.py:328
  67.9 1.4 %collective-permute-start.10 = (bf16[512,128]{1,0:T(8,128)(2,1)S(1)}, bf16[512,128]{1,0:T(8,128)(2,1)S(1)}, u32[]{:S(2)}, u32[]{:S(2)}) collective-permute-start(bf16[512,128]{1,0:T(8,128)(2,1)S(1)} %bitcast.10), channel_id=1, source_target_pairs={{0,64},{8,72},{16,80},{24,88},{32,96},{40,104},{48,112},{56,120},{... | collective-permute-start | bytes 393224 | tf_op jit(solution)/shard_map/ppermute | solution.py:328
  69.4 1.4 %shard_map.87 = f32[2048,128]{1,0:T(8,128)} custom-call(bf16[2048,128]{1,0:T(8,128)(2,1)S(1)} %get-tuple-element.40.sent_ref, f32[2048,128]{1,0:T(8,128)S(1)} %get-tuple-element.31.base_ref, bf16[1024,128]{1,0:T(8,128)(2,1)S(1)} %collective-permute-done.7.low_ref, bf16[1024,128]{1,0:T(8,128)(2,1)S(1)} %collective-permute-done.9.high_ref, ...), custom_call_target="tpu_custom_call" | custom-call | bytes 2228224 | tf_op jit(solution)/shard_map/pallas_call | solution.py:87
  70.8 0.7 collective-permute-done.12.refs_3_
  71.4 1.5 %collective-permute-done.11.refs_2_ = bf16[512,128]{1,0:T(8,128)(2,1)S(1)} collective-permute-done((bf16[512,128]{1,0:T(8,128)(2,1)S(1)}, bf16[512,128]{1,0:T(8,128)(2,1)S(1)}, u32[]{:S(2)}, u32[]{:S(2)}) %collective-permute-start.11) | collective-permute-done | bytes 131104 | tf_op jit(solution)/shard_map/ppermute | solution.py:328
  72.9 0.8 %collective-permute-done.10.refs_1_ = bf16[512,128]{1,0:T(8,128)(2,1)S(1)} collective-permute-done((bf16[512,128]{1,0:T(8,128)(2,1)S(1)}, bf16[512,128]{1,0:T(8,128)(2,1)S(1)}, u32[]{:S(2)}, u32[]{:S(2)}) %collective-permute-start.10) | collective-permute-done | bytes 131104 | tf_op jit(solution)/shard_map/ppermute | solution.py:328
  73.7 1.1 %shard_map.89 = f32[2048,128]{1,0:T(8,128)} custom-call(bf16[512,128]{1,0:T(8,128)(2,1)S(1)} %bitcast.11, bf16[512,128]{1,0:T(8,128)(2,1)S(1)} %collective-permute-done.10.refs_1_, bf16[512,128]{1,0:T(8,128)(2,1)S(1)} %collective-permute-done.11.refs_2_, bf16[512,128]{1,0:T(8,128)(2,1)S(1)} %collective-permute-done.12.refs_3_), custom_call_target="tpu_custom_call" | custom-call | bytes 524288 | tf_op jit(solution)/shard_map/pallas_call | solution.py:87
  (21 shorter events, 0.4 us)
Async XLA Ops:
  0.6 3.4 %copy-start = (bf16[1,1,2097152]{2,1,0:T(2,128)(2,1)S(1)}, bf16[1,1,2097152]{2,1,0:T(2,128)(2,1)}, u32[]{:S(2)}) copy-start(bf16[1,1,2097152]{2,1,0:T(2,128)(2,1)} %raw_ref.3) | copy-start | bytes 12582916
  4.1 17.0 %copy-start.4 = (s32[1,512,32]{1,2,0:T(8,128)S(1)}, s32[1,512,32]{1,2,0:T(8,128)}, u32[]{:S(2)}) copy-start(s32[1,512,32]{1,2,0:T(8,128)} %param.8) | copy-start | bytes 196612
  4.1 17.0 %copy-start.5 = (s32[1,512]{1,0:T(1,128)S(1)}, s32[1,512]{1,0:T(1,128)}, u32[]{:S(2)}) copy-start(s32[1,512]{1,0:T(1,128)} %counts_ref.1) | copy-start | bytes 6148
  4.1 19.0 %copy-start.1 = (bf16[256,256]{1,0:T(8,128)(2,1)S(1)}, bf16[256,256]{1,0:T(8,128)(2,1)}, u32[]{:S(2)}) copy-start(bf16[256,256]{1,0:T(8,128)(2,1)} %constant.4.clone.fwd_ref) | copy-start | bytes 393220
  4.1 19.0 %copy-start.2 = (bf16[256,256]{1,0:T(8,128)(2,1)S(1)}, bf16[256,256]{1,0:T(8,128)(2,1)}, u32[]{:S(2)}) copy-start(bf16[256,256]{1,0:T(8,128)(2,1)} %constant.5.clone.inv_ref.refs_1_) | copy-start | bytes 393220
  4.1 19.0 %copy-start.3 = (f32[1,262144]{1,0:T(1,128)S(1)}, f32[1,262144]{1,0:T(1,128)}, u32[]{:S(2)}) copy-start(f32[1,262144]{1,0:T(1,128)} %param.7) | copy-start | bytes 3145732
  4.1 2.0 %collective-permute-start.5 = (bf16[2048,128]{1,0:T(8,128)(2,1)S(1)}, bf16[2048,128]{1,0:T(8,128)(2,1)S(1)}, u32[]{:S(2)}, u32[]{:S(2)}) collective-permute-start(bf16[2048,128]{1,0:T(8,128)(2,1)S(1)} %shard_map.82), channel_id=1, source_target_pairs={{0,1},{1,0},{2,3},{3,2},{4,5},{5,4},{6,7},{7,6},{8,9},{9,8},{10,11... | collective-permute-start | bytes 1572872 | tf_op jit(solution)/shard_map/ppermute | solution.py:250
  4.8 3.6 %collective-permute-start.1 = (bf16[2048,128]{1,0:T(8,128)(2,1)S(1)}, bf16[2048,128]{1,0:T(8,128)(2,1)S(1)}, u32[]{:S(2)}, u32[]{:S(2)}) collective-permute-start(bf16[2048,128]{1,0:T(8,128)(2,1)S(1)} %get-tuple-element.25), channel_id=1, source_target_pairs={{0,1},{1,0},{2,3},{3,2},{4,5},{5,4},{6,7},{7,6},{8,9},{9,8},{10,11... | collective-permute-start | bytes 1572872 | tf_op jit(solution)/shard_map/ppermute | solution.py:250
  5.3 3.1 %collective-permute-start.2 = (bf16[2048,128]{1,0:T(8,128)(2,1)S(1)}, bf16[2048,128]{1,0:T(8,128)(2,1)S(1)}, u32[]{:S(2)}, u32[]{:S(2)}) collective-permute-start(bf16[2048,128]{1,0:T(8,128)(2,1)S(1)} %get-tuple-element.27), channel_id=1, source_target_pairs={{0,1},{1,0},{2,3},{3,2},{4,5},{5,4},{6,7},{7,6},{8,9},{9,8},{10,11... | collective-permute-start | bytes 1572872 | tf_op jit(solution)/shard_map/ppermute | solution.py:250
  5.4 16.2 %collective-permute-start = (bf16[2048,128]{1,0:T(8,128)(2,1)S(1)}, bf16[2048,128]{1,0:T(8,128)(2,1)S(1)}, u32[]{:S(2)}, u32[]{:S(2)}) collective-permute-start(bf16[2048,128]{1,0:T(8,128)(2,1)S(1)} %get-tuple-element.23), channel_id=1, source_target_pairs={{0,1},{1,0},{2,3},{3,2},{4,5},{5,4},{6,7},{7,6},{8,9},{9,8},{10,11... | collective-permute-start | bytes 1572872 | tf_op jit(solution)/shard_map/ppermute | solution.py:250
  6.3 9.2 %collective-permute-start.6 = (bf16[1024,128]{1,0:T(8,128)(2,1)S(1)}, bf16[1024,128]{1,0:T(8,128)(2,1)S(1)}, u32[]{:S(2)}, u32[]{:S(2)}) collective-permute-start(bf16[1024,128]{1,0:T(8,128)(2,1)S(1)} %get-tuple-element.34), channel_id=1, source_target_pairs={{0,2},{1,3},{2,0},{3,1},{4,6},{5,7},{6,4},{7,5},{8,10},{9,11},{10,... | collective-permute-start | bytes 786440 | tf_op jit(solution)/shard_map/ppermute | solution.py:253
  7.1 10.5 %collective-permute-start.8 = (bf16[1024,128]{1,0:T(8,128)(2,1)S(1)}, bf16[1024,128]{1,0:T(8,128)(2,1)S(1)}, u32[]{:S(2)}, u32[]{:S(2)}) collective-permute-start(bf16[1024,128]{1,0:T(8,128)(2,1)S(1)} %get-tuple-element.36), channel_id=1, source_target_pairs={{0,6},{1,7},{2,4},{3,5},{4,2},{5,3},{6,0},{7,1},{8,14},{9,15},{10,... | collective-permute-start | bytes 786440 | tf_op jit(solution)/shard_map/ppermute | solution.py:253
  8.6 12.5 %collective-permute-start.3 = (bf16[1024,128]{1,0:T(8,128)(2,1)S(1)}, bf16[1024,128]{1,0:T(8,128)(2,1)S(1)}, u32[]{:S(2)}, u32[]{:S(2)}) collective-permute-start(bf16[1024,128]{1,0:T(8,128)(2,1)S(1)} %get-tuple-element.28), channel_id=1, source_target_pairs={{0,2},{1,3},{2,0},{3,1},{4,6},{5,7},{6,4},{7,5},{8,10},{9,11},{10,... | collective-permute-start | bytes 786440 | tf_op jit(solution)/shard_map/ppermute | solution.py:253
  10.1 13.1 %collective-permute-start.4 = (bf16[1024,128]{1,0:T(8,128)(2,1)S(1)}, bf16[1024,128]{1,0:T(8,128)(2,1)S(1)}, u32[]{:S(2)}, u32[]{:S(2)}) collective-permute-start(bf16[1024,128]{1,0:T(8,128)(2,1)S(1)} %get-tuple-element.29), channel_id=1, source_target_pairs={{0,6},{1,7},{2,4},{3,5},{4,2},{5,3},{6,0},{7,1},{8,14},{9,15},{10,... | collective-permute-start | bytes 786440 | tf_op jit(solution)/shard_map/ppermute | solution.py:253
  15.6 12.1 %collective-permute-start.7 = (bf16[1024,128]{1,0:T(8,128)(2,1)S(1)}, bf16[1024,128]{1,0:T(8,128)(2,1)S(1)}, u32[]{:S(2)}, u32[]{:S(2)}) collective-permute-start(bf16[1024,128]{1,0:T(8,128)(2,1)S(1)} %shard_map.84), channel_id=1, source_target_pairs={{0,6},{1,7},{2,4},{3,5},{4,2},{5,3},{6,0},{7,1},{8,14},{9,15},{10,... | collective-permute-start | bytes 786440 | tf_op jit(solution)/shard_map/ppermute | solution.py:253
  17.7 10.0 %collective-permute-start.9 = (bf16[1024,128]{1,0:T(8,128)(2,1)S(1)}, bf16[1024,128]{1,0:T(8,128)(2,1)S(1)}, u32[]{:S(2)}, u32[]{:S(2)}) collective-permute-start(bf16[1024,128]{1,0:T(8,128)(2,1)S(1)} %shard_map.85), channel_id=1, source_target_pairs={{0,2},{1,3},{2,0},{3,1},{4,6},{5,7},{6,4},{7,5},{8,10},{9,11},{10,... | collective-permute-start | bytes 786440 | tf_op jit(solution)/shard_map/ppermute | solution.py:253
  65.3 6.2 %collective-permute-start.12 = (bf16[512,128]{1,0:T(8,128)(2,1)S(1)}, bf16[512,128]{1,0:T(8,128)(2,1)S(1)}, u32[]{:S(2)}, u32[]{:S(2)}) collective-permute-start(bf16[512,128]{1,0:T(8,128)(2,1)S(1)} %bitcast.8), channel_id=1, source_target_pairs={{0,192},{8,200},{16,208},{24,216},{32,224},{40,232},{48,240},{56,2... | collective-permute-start | bytes 393224 | tf_op jit(solution)/shard_map/ppermute | solution.py:328
  66.4 6.5 %collective-permute-start.11 = (bf16[512,128]{1,0:T(8,128)(2,1)S(1)}, bf16[512,128]{1,0:T(8,128)(2,1)S(1)}, u32[]{:S(2)}, u32[]{:S(2)}) collective-permute-start(bf16[512,128]{1,0:T(8,128)(2,1)S(1)} %bitcast.9), channel_id=1, source_target_pairs={{0,128},{8,136},{16,144},{24,152},{32,160},{40,168},{48,176},{56,1... | collective-permute-start | bytes 393224 | tf_op jit(solution)/shard_map/ppermute | solution.py:328
  67.9 5.8 %collective-permute-start.10 = (bf16[512,128]{1,0:T(8,128)(2,1)S(1)}, bf16[512,128]{1,0:T(8,128)(2,1)S(1)}, u32[]{:S(2)}, u32[]{:S(2)}) collective-permute-start(bf16[512,128]{1,0:T(8,128)(2,1)S(1)} %bitcast.10), channel_id=1, source_target_pairs={{0,64},{8,72},{16,80},{24,88},{32,96},{40,104},{48,112},{56,120},{... | collective-permute-start | bytes 393224 | tf_op jit(solution)/shard_map/ppermute | solution.py:328
